TPU v7x, 256 devices: a whole 4x4x8 slice. The times are simulated.
256 devices in a mesh: ao: 128 (over x, z, y), aux: 2 (over core).
Axes of the slice: x: 4, y: 4, z: 8, core: 2. Of those that a mesh axis runs over, the one named last changes fastest.
Arguments:
- factors: bfloat16 [2, 196608, 3000], P('aux', 'ao'), may hold values from -1.75 to 1.75
- pair_keep: int32 [768, 2], P('ao'), may hold values 0 or 1
Outputs:
- upper_band: float32 [196608, 768], P(('ao', 'aux'))
- lower_band: float32 [196608, 512], P(('ao', 'aux'))
All inputs are finite; a program needn't handle non-finite values. No bound on the sum of `pair_keep` on one device may be relied on, other than what follows from the above.
Results may differ from a plain program's by a relative error of at most 0.0003.
Values may be sent and summed in bfloat16 or wider, within the bound.
No kernel may reach another device: no remote copies, remote signals or barrier semaphores. Data moves between devices by JAX's collectives and lax.ppermute only.
A program may use at most 128 MiB of HBM per device.

v0:
```python
import jax
import jax.numpy as jnp
from jax import lax
from jax.sharding import PartitionSpec as P


def from_behind(block, axis, distance):
    devices = range(lax.axis_size(axis))
    route = [(i - distance, i) for i in devices if i - distance in devices]
    return lax.ppermute(block, axis, route)


def body(factors, pair_keep):
    aux_rows, all_rows, nocc = factors.shape
    blocks_here, partners = pair_keep.shape
    width = all_rows // blocks_here
    own = factors.reshape(aux_rows, blocks_here, width, nocc)

    def pair_tile(operands):
        return jnp.einsum(
            "pai,pbi->ab", operands[0], operands[1], preferred_element_type=jnp.float32
        )

    def empty_tile(operands):
        return jnp.zeros((width, width), jnp.float32)

    def masked_tile(flag, left, right):
        return lax.cond(flag, pair_tile, empty_tile, (left, right))

    tiles = {}
    for block in range(blocks_here):
        tiles[block, 0] = pair_tile((own[:, block], own[:, block]))
        for offset in range(1, partners + 1):
            if block + offset < blocks_here:
                tiles[block, offset] = masked_tile(
                    pair_keep[block, offset - 1] > 0, own[:, block], own[:, block + offset]
                )
    crossing = []
    for block in range(partners):
        for offset in range(block + 1, partners + 1):
            crossing.append((block, offset))
    incoming = {}
    edge = from_behind(own[:, :partners], "ao", -1)
    for block, offset in crossing:
        source = blocks_here + block - offset
        tiles[source, offset] = masked_tile(
            pair_keep[source, offset - 1] > 0, own[:, source], edge[:, block]
        )
    outgoing = jnp.stack(
        [tiles[blocks_here + block - offset, offset].T for block, offset in crossing], axis=0
    )
    received = from_behind(outgoing, "ao", 1)
    for position, key in enumerate(crossing):
        incoming[key] = received[position]
    upper_rows = []
    lower_rows = []
    for block in range(blocks_here):
        upper_rows.append(
            jnp.concatenate([tiles[block, offset] for offset in range(partners + 1)], axis=1)
        )
        pieces = []
        for offset in range(1, partners + 1):
            if block - offset >= 0:
                pieces.append(tiles[block - offset, offset].T)
            else:
                pieces.append(incoming[block, offset])
        lower_rows.append(jnp.concatenate(pieces, axis=1))
    upper_local = jnp.concatenate(upper_rows, axis=0)
    lower_local = jnp.concatenate(lower_rows, axis=0)
    upper_band, lower_band = (
        lax.psum_scatter(upper_local, "aux", scatter_dimension=0, tiled=True),
        lax.psum_scatter(lower_local, "aux", scatter_dimension=0, tiled=True),
    )
    return (upper_band, lower_band)


def solution(mesh):
    in_specs = (P("aux", "ao", None), P("ao", None))
    out_specs = (P(("ao", "aux"), None), P(("ao", "aux"), None))
    return jax.shard_map(body, mesh=mesh, in_specs=in_specs, out_specs=out_specs, check_vma=False)
```

profile of v0, /device:TPU:6, one launch (start us, length us, event | category | flops | bytes accessed | tf_op | source)
XLA Modules:
  0.0 165.5 jit_solution(10854120116207363148)
XLA Ops:
  7.2 12.8 %copy.79 = bf16[1,1536,3000]{2,1,0:T(8,128)(2,1)} copy(bf16[1,1536,3000]{1,2,0:T(8,128)(2,1)} %param.26) | data formatting | bytes 18432000 | tf_op args[0]
  20.0 2.1 %slice.131 = bf16[1,2,256,3000]{3,2,1,0:T(8,128)(2,1)S(1)} slice(bf16[1,6,256,3000]{3,2,1,0:T(8,128)(2,1)} %bitcast.143), slice={[0:1], [0:2], [0:256], [0:3000]} | slice | bytes 6144000 | tf_op jit(solution)/shard_map/slice | solution.py:43
  22.1 3.0 %copy.88 = bf16[1,2,256,3000]{2,3,1,0:T(8,128)(2,1)} copy(bf16[1,2,256,3000]{3,2,1,0:T(8,128)(2,1)S(1)} %slice.131) | data formatting | bytes 6144000 | tf_op jit(solution)/shard_map/slice | solution.py:43
  25.0 10.5 %collective-permute-start = (bf16[1,2,256,3000]{2,3,1,0:T(8,128)(2,1)}, bf16[1,2,256,3000]{2,3,1,0:T(8,128)(2,1)}, u32[]{:S(2)}, u32[]{:S(2)}) collective-permute-start(bf16[1,2,256,3000]{2,3,1,0:T(8,128)(2,1)} %copy.88), channel_id=1, source_target_pairs={{2,0},{4,2},{6,4},{8,6},{10,8},{12,10},{14,12},{16,14},{18,16},{20... | collective-permute-start | bytes 9216008 | tf_op jit(solution)/shard_map/ppermute | solution.py:10
  35.5 6.5 %slice_bitcast_fusion.3 = (bf16[1,256,3000]{2,1,0:T(8,128)(2,1)}, bf16[1,256,3000]{2,1,0:T(8,128)(2,1)}, bf16[1,256,3000]{2,1,0:T(8,128)(2,1)S(1)}, bf16[1,256,3...) fusion(bf16[1,6,256,3000]{3,2,1,0:T(8,128)(2,1)} %bitcast.144), kind=kLoop, calls=%fused_computation.50 | loop fusion | bytes 18432000 | tf_op jit(solution)/shard_map/squeeze | solution.py:36
  50.2 2.0 %conditional.16 = (f32[256,256]{0,1:T(8,128)S(1)}) conditional(s32[]{:T(128)} %bitcast.36, () %tuple.88, (bf16[1,256,3000]{2,1,0:T(8,128)(2,1)S(1)}, bf16[1,256,3000]{2,1,0:T(8,128)(2,1)}) %tuple.89), branch_computations={%region_8.0_spmd, %region_9.0_spmd} | conditional | flops 393216000 | bytes 3334152 | solution.py:28
  58.0 2.5 %conditional.15 = (f32[256,256]{0,1:T(8,128)S(1)}) conditional(s32[]{:T(128)} %bitcast.33, () %tuple.86, (bf16[1,256,3000]{2,1,0:T(8,128)(2,1)}, bf16[1,256,3000]{2,1,0:T(8,128)(2,1)}) %tuple.87), branch_computations={%region_6.0_spmd, %region_7.0_spmd} | conditional | flops 393216000 | bytes 3334152 | solution.py:28
  58.0 2.5 %fusion.9 = f32[256,256]{0,1:T(8,128)S(1)} fusion(bf16[1,256,3000]{2,1,0:T(8,128)(2,1)} %get-tuple-element.90, bf16[1,256,3000]{2,1,0:T(8,128)(2,1)} %get-tuple-element.88), kind=kOutput, calls=%fused_computation.9 | convolution fusion | flops 393216000 | bytes 3334144 | tf_op jit(solution)/shard_map/cond | solution.py:28
  61.9 2.7 %conditional.13 = (f32[256,256]{0,1:T(8,128)}) conditional(s32[]{:T(128)} %bitcast.29, () %tuple.82, (bf16[1,256,3000]{2,1,0:T(8,128)(2,1)}, bf16[1,256,3000]{2,1,0:T(8,128)(2,1)S(1)}) %tuple.83), branch_computations={%region_2.0_spmd, %region_3.0_spmd} | conditional | flops 393216000 | bytes 3334152 | solution.py:28
  61.9 2.7 %fusion.3 = f32[256,256]{0,1:T(8,128)} fusion(bf16[1,256,3000]{2,1,0:T(8,128)(2,1)S(1)} %get-tuple-element.82, bf16[1,256,3000]{2,1,0:T(8,128)(2,1)} %get-tuple-element.80), kind=kOutput, calls=%fused_computation.3 | convolution fusion | flops 393216000 | bytes 3334144 | tf_op jit(solution)/shard_map/cond | solution.py:28
  64.7 2.6 %fusion.45 = f32[256,256]{0,1:T(8,128)S(1)} fusion(bf16[1,6,256,3000]{3,2,1,0:T(8,128)(2,1)} %bitcast.145), kind=kOutput, calls=%fused_computation.46 | convolution fusion | flops 393216000 | bytes 1835008 | tf_op jit(solution)/shard_map/pai,pbi->ab/dot_general | solution.py:20
  68.3 2.5 %fusion.43 = f32[256,256]{0,1:T(8,128)S(1)} fusion(bf16[1,6,256,3000]{3,2,1,0:T(8,128)(2,1)} %bitcast.146), kind=kOutput, calls=%fused_computation.44 | convolution fusion | flops 393216000 | bytes 1835008 | tf_op jit(solution)/shard_map/pai,pbi->ab/dot_general | solution.py:20
  71.0 2.6 %fusion.41 = f32[256,256]{0,1:T(8,128)S(1)} fusion(bf16[1,6,256,3000]{3,2,1,0:T(8,128)(2,1)} %bitcast.147), kind=kOutput, calls=%fused_computation.42 | convolution fusion | flops 393216000 | bytes 1835008 | tf_op jit(solution)/shard_map/pai,pbi->ab/dot_general | solution.py:20
  73.7 2.5 %fusion.39 = f32[256,256]{0,1:T(8,128)S(1)} fusion(bf16[1,6,256,3000]{3,2,1,0:T(8,128)(2,1)} %bitcast.148), kind=kOutput, calls=%fused_computation.40 | convolution fusion | flops 393216000 | bytes 1835008 | tf_op jit(solution)/shard_map/pai,pbi->ab/dot_general | solution.py:20
  76.4 4.9 %fusion.35 = f32[256,256]{0,1:T(8,128)} fusion(bf16[1,6,256,3000]{3,2,1,0:T(8,128)(2,1)} %bitcast.149), kind=kOutput, calls=%fused_computation.36 | convolution fusion | flops 393216000 | bytes 1835008 | tf_op jit(solution)/shard_map/pai,pbi->ab/dot_general | solution.py:20
  81.3 3.3 %fusion.37 = f32[256,256]{0,1:T(8,128)} fusion(bf16[1,6,256,3000]{3,2,1,0:T(8,128)(2,1)} %bitcast.150), kind=kOutput, calls=%fused_computation.38 | convolution fusion | flops 393216000 | bytes 1835008 | tf_op jit(solution)/shard_map/pai,pbi->ab/dot_general | solution.py:20
  84.6 17.0 %collective-permute-done = bf16[1,2,256,3000]{2,3,1,0:T(8,128)(2,1)} collective-permute-done((bf16[1,2,256,3000]{2,3,1,0:T(8,128)(2,1)}, bf16[1,2,256,3000]{2,3,1,0:T(8,128)(2,1)}, u32[]{:S(2)}, u32[]{:S(2)}) %collective-permute-start) | collective-permute-done | bytes 3072032 | tf_op jit(solution)/shard_map/ppermute | solution.py:10
  101.6 2.6 %slice_bitcast_fusion.2 = bf16[1,256,3000]{1,2,0:T(8,128)(2,1)} fusion(bf16[1,2,256,3000]{2,3,1,0:T(8,128)(2,1)} %collective-permute-done), kind=kLoop, calls=%fused_computation.48 | loop fusion | bytes 3072000 | tf_op jit(solution)/shard_map/squeeze | solution.py:47
  105.7 2.1 %conditional.21 = (f32[256,256]{0,1:T(8,128)S(1)}) conditional(s32[]{:T(128)} %bitcast.45, () %tuple.98, (bf16[1,256,3000]{2,1,0:T(8,128)(2,1)S(1)}, bf16[1,256,3000]{1,2,0:T(8,128)(2,1)}) %tuple.99), branch_computations={%region_18.0_spmd, %region_19.0_spmd} | conditional | flops 393216000 | bytes 3334152 | solution.py:28
  105.7 2.1 %fusion.27 = f32[256,256]{0,1:T(8,128)S(1)} fusion(bf16[1,256,3000]{2,1,0:T(8,128)(2,1)S(1)} %get-tuple-element.104, bf16[1,256,3000]{1,2,0:T(8,128)(2,1)} %get-tuple-element.141), kind=kOutput, calls=%fused_computation.27 | convolution fusion | flops 393216000 | bytes 3334144 | tf_op jit(solution)/shard_map/cond | solution.py:28
  112.0 4.3 %collective-permute-start.1 = (f32[3,256,256]{2,1,0:T(8,128)S(1)}, f32[3,256,256]{2,1,0:T(8,128)S(1)}, u32[]{:S(2)}, u32[]{:S(2)}) collective-permute-start(f32[3,256,256]{2,1,0:T(8,128)S(1)} %pad_maximum_fusion), channel_id=1, source_target_pairs={{0,2},{2,4},{4,6},{6,8},{8,10},{10,12},{12,14},{14,16},{16,18},{18... | collective-permute-start | bytes 2359304 | tf_op jit(solution)/shard_map/ppermute | solution.py:10
  116.3 26.0 %collective-permute-done.1 = f32[3,256,256]{2,1,0:T(8,128)S(1)} collective-permute-done((f32[3,256,256]{2,1,0:T(8,128)S(1)}, f32[3,256,256]{2,1,0:T(8,128)S(1)}, u32[]{:S(2)}, u32[]{:S(2)}) %collective-permute-start.1) | collective-permute-done | bytes 786464 | tf_op jit(solution)/shard_map/ppermute | solution.py:10
  145.5 3.0 %copy.108 = f32[768,768]{1,0:T(8,128)} copy(f32[768,768]{0,1:T(8,128)} %reduce-scatter.3.cloned.1.call-done) | data formatting | bytes 4718592
  148.5 10.1 %reduce-scatter.5.cloned.1.call-done = f32[768,512]{1,0:T(8,128)} async-done(((f32[1536,512]{1,0:T(8,128)}), f32[768,512]{1,0:T(8,128)}) %reduce-scatter.5.cloned.1.call-update) | async-done | bytes 1572880 | tf_op jit(solution)/shard_map/reduce_scatter | solution.py:72
  (95 shorter events, 22.6 us)
Async XLA Ops:
  7.2 138.3 %reduce-scatter.3.cloned.1.call-start = ((), (), s32[]{:S(2)}) async-start(), calls=%async_computation.2 | async-start | bytes 7077888 | tf_op jit(solution)/shard_map/reduce_scatter | solution.py:71
  25.0 76.5 %collective-permute-start = (bf16[1,2,256,3000]{2,3,1,0:T(8,128)(2,1)}, bf16[1,2,256,3000]{2,3,1,0:T(8,128)(2,1)}, u32[]{:S(2)}, u32[]{:S(2)}) collective-permute-start(bf16[1,2,256,3000]{2,3,1,0:T(8,128)(2,1)} %copy.88), channel_id=1, source_target_pairs={{2,0},{4,2},{6,4},{8,6},{10,8},{12,10},{14,12},{16,14},{18,16},{20... | collective-permute-start | bytes 9216008 | tf_op jit(solution)/shard_map/ppermute | solution.py:10
  35.5 6.5 %copy-start.28 = (s32[6,2]{0,1:T(2,128)S(1)}, s32[6,2]{0,1:T(2,128)}, u32[]{:S(2)}) copy-start(s32[6,2]{0,1:T(2,128)} %param.27) | copy-start | bytes 148
  64.7 2.6 %copy-start.22 = (f32[256,256]{0,1:T(8,128)S(1)}, f32[256,256]{0,1:T(8,128)}, u32[]{:S(2)}) copy-start(f32[256,256]{0,1:T(8,128)} %copy-done.21) | copy-start | bytes 786436
  68.3 2.6 %copy-start.16 = (f32[256,256]{0,1:T(8,128)S(1)}, f32[256,256]{0,1:T(8,128)}, u32[]{:S(2)}) copy-start(f32[256,256]{0,1:T(8,128)} %copy-done.15) | copy-start | bytes 786436
  68.3 2.6 %copy-start.19 = (f32[256,256]{0,1:T(8,128)S(1)}, f32[256,256]{0,1:T(8,128)}, u32[]{:S(2)}) copy-start(f32[256,256]{0,1:T(8,128)} %copy-done.18) | copy-start | bytes 786436
  71.0 2.6 %copy-start.4 = (f32[256,256]{0,1:T(8,128)S(1)}, f32[256,256]{0,1:T(8,128)}, u32[]{:S(2)}) copy-start(f32[256,256]{0,1:T(8,128)} %copy-done.3) | copy-start | bytes 786436
  73.7 2.6 %copy-start.7 = (f32[256,256]{0,1:T(8,128)S(1)}, f32[256,256]{0,1:T(8,128)}, u32[]{:S(2)}) copy-start(f32[256,256]{0,1:T(8,128)} %copy-done.6) | copy-start | bytes 786436
  73.7 2.6 %copy-start.10 = (f32[256,256]{0,1:T(8,128)S(1)}, f32[256,256]{0,1:T(8,128)}, u32[]{:S(2)}) copy-start(f32[256,256]{0,1:T(8,128)} %copy-done.9) | copy-start | bytes 786436
  76.4 27.8 %copy-start.1 = (f32[1536,768]{0,1:T(8,128)}, f32[1536,768]{0,1:T(8,128)S(1)}, u32[]{:S(2)}) copy-start(f32[1536,768]{0,1:T(8,128)S(1)} %maximum_dynamic-update-slice_fusion.2) | copy-start | bytes 14155780
  84.6 19.6 %copy-start = (bf16[1,256,3000]{2,1,0:T(8,128)(2,1)S(1)}, bf16[1,256,3000]{2,1,0:T(8,128)(2,1)}, u32[]{:S(2)}) copy-start(bf16[1,256,3000]{2,1,0:T(8,128)(2,1)} %get-tuple-element.160) | copy-start | bytes 4608004
  105.0 2.8 %copy-start.13 = (f32[256,256]{0,1:T(8,128)S(1)}, f32[256,256]{0,1:T(8,128)}, u32[]{:S(2)}) copy-start(f32[256,256]{0,1:T(8,128)} %copy-done.12) | copy-start | bytes 786436
  105.0 2.8 %copy-start.27 = (f32[256,256]{0,1:T(8,128)S(1)}, f32[256,256]{0,1:T(8,128)}, u32[]{:S(2)}) copy-start(f32[256,256]{0,1:T(8,128)} %fusion.37) | copy-start | bytes 786436
  107.8 1.1 copy-start.26
  110.9 47.8 %reduce-scatter.5.cloned.1.call-start = ((), (), s32[]{:S(2)}) async-start(), calls=%async_computation.3 | async-start | bytes 4718592 | tf_op jit(solution)/shard_map/reduce_scatter | solution.py:72
  112.0 30.4 %copy-start.23 = (f32[256,256]{0,1:T(8,128)S(1)}, f32[256,256]{0,1:T(8,128)}, u32[]{:S(2)}) copy-start(f32[256,256]{0,1:T(8,128)} %copy-done.21) | copy-start | bytes 786436
  112.0 30.5 %copy-start.17 = (f32[256,256]{0,1:T(8,128)S(1)}, f32[256,256]{0,1:T(8,128)}, u32[]{:S(2)}) copy-start(f32[256,256]{0,1:T(8,128)} %copy-done.15) | copy-start | bytes 786436
  112.0 30.3 %collective-permute-start.1 = (f32[3,256,256]{2,1,0:T(8,128)S(1)}, f32[3,256,256]{2,1,0:T(8,128)S(1)}, u32[]{:S(2)}, u32[]{:S(2)}) collective-permute-start(f32[3,256,256]{2,1,0:T(8,128)S(1)} %pad_maximum_fusion), channel_id=1, source_target_pairs={{0,2},{2,4},{4,6},{6,8},{8,10},{10,12},{12,14},{14,16},{16,18},{18... | collective-permute-start | bytes 2359304 | tf_op jit(solution)/shard_map/ppermute | solution.py:10
  142.3 1.3 copy-start.20
  142.4 1.3 copy-start.5
  142.4 1.3 copy-start.8
  142.5 1.2 copy-start.11
  142.5 1.2 copy-start.14
  143.8 1.6 copy-start.2
  (9 other events, 6.7 us)
Sparse Core Ops, SparseCore 0:
  111.0 24.6 reduce-scatter.2
  145.6 13.0 reduce-scatter.4
where the time goes:
time: 168 us; the launch traced here: 166 us
  waiting for transfers between devices  53.2 us (32%)
  local copies, waits for them, and re-layouts  39 us (23%)
  matrix products  29.8 us (18%)
  between operations  22.1 us (13%)
  starting transfers between devices  14.8 us (9%)
  other arithmetic  6.53 us (4%)
    ppermute x2, waiting for transfers between devices, from_behind(): return lax.ppermute(block, axis, route)  43 us
    unnamed x60, local copies, waits for them, and re-layouts  23.3 us
    dot_general x6, matrix products, pair_tile(): jnp.einsum('pai,pbi->ab', operands[0], operands[1], preferred_element_typ...  18.5 us
    ppermute x2, starting transfers between devices, from_behind(): return lax.ppermute(block, axis, route)  14.7 us
    cond x5, matrix products, masked_tile(): return lax.cond(flag, pair_tile, empty_tile, (left, right))  11.4 us
    reduce_scatter x1, waiting for transfers between devices, body(): lax.psum_scatter(lower_local, 'aux', scatter_dimension=0, tiled=True)  10.1 us
    squeeze x1, local copies, waits for them, and re-layouts, body(): own[:, block + offset]  6.5 us
    slice x2, local copies, waits for them, and re-layouts, body(): edge = from_behind(own[:, :partners], 'ao', -1)  5.06 us
  transfers between devices with their start and end apart: 4, of which 3 were waited for; matrix products, arithmetic and copies ran while one was open for 25% of the time, Pallas kernels for 0%

commit v1 on v0

v1 whole, which is shorter than its diff:
```python
import functools

import jax
import jax.numpy as jnp
import numpy as np
from jax import lax
from jax.experimental import pallas as pl
from jax.experimental.pallas import tpu as pltpu
from jax.sharding import PartitionSpec as P

BS = 256
BLOCKS = 6
HALF = 128

KEPT = (
    ((0, 0), (0, 1), (0, 2), (1, 1), (1, 2), (2, 2), (1, 3), (2, 3), (2, 4)),
    ((1, 3), (2, 3), (2, 4), (3, 3), (3, 4), (3, 5), (4, 4), (4, 5), (5, 5)),
)
SLOTS = 9


def slot_table():
    table = np.full((2, 2, BLOCKS, 3), -1, np.int32)
    for core in range(2):
        for whose in range(2):
            for slot, (m, n) in enumerate(KEPT[core if whose == 0 else 1 - core]):
                table[core, whose, n, m - n + 2] = slot
    return table


def local_kernel(table, g_ref, keep_ref, give_ref, wide_ref, turned):
    n = pl.program_id(0)
    rows = pl.multiple_of((n + 2) * BS, BS)
    flipped = g_ref[...].T
    turned[pl.ds(rows, BS), :] = flipped

    @pl.when(n < 2)
    def _():
        wide_ref[pl.ds(pl.multiple_of((n + 2) * BS, BS), BS), :] = flipped

    @pl.when(n > 3)
    def _():
        wide_ref[pl.ds(pl.multiple_of((n - 4) * BS, BS), BS), :] = flipped

    left = turned[pl.ds(pl.multiple_of(n * BS, BS), 3 * BS), :]
    tiles = jnp.dot(left, g_ref[...], preferred_element_type=jnp.float32)
    for k in range(3):
        tile = tiles[k * BS:(k + 1) * BS]
        for whose, out in ((0, keep_ref), (1, give_ref)):
            slot = table[(whose * BLOCKS + n) * 3 + k]

            @pl.when(slot >= 0)
            def _():
                out[slot] = tile


def local_tiles(core, g):
    table = jnp.asarray(slot_table())[core].reshape(-1)
    nocc = g.shape[0]
    return pl.pallas_call(
        local_kernel,
        grid_spec=pltpu.PrefetchScalarGridSpec(
            num_scalar_prefetch=1,
            grid=(BLOCKS,),
            in_specs=[pl.BlockSpec((nocc, BS), lambda n, t: (0, n))],
            out_specs=[
                pl.BlockSpec((SLOTS, BS, BS), lambda n, t: (0, 0, 0)),
                pl.BlockSpec((SLOTS, BS, BS), lambda n, t: (0, 0, 0)),
                pl.BlockSpec((4 * BS, nocc), lambda n, t: (0, 0)),
            ],
            scratch_shapes=[pltpu.VMEM(((BLOCKS + 2) * BS, nocc), jnp.bfloat16)],
        ),
        out_shape=[
            jax.ShapeDtypeStruct((SLOTS, BS, BS), jnp.float32),
            jax.ShapeDtypeStruct((SLOTS, BS, BS), jnp.float32),
            jax.ShapeDtypeStruct((4 * BS, nocc), jnp.bfloat16),
        ],
        compiler_params=pltpu.CompilerParams(vmem_limit_bytes=48 * 1024 * 1024),
        cost_estimate=pl.CostEstimate(
            flops=7_000_000_000, bytes_accessed=20_000_000, transcendentals=0
        ),
        name="local_tiles",
    )(table, g)


def edge_kernel(core, wide_ref, down_ref, up_ref, own_ref, give_ref):
    low = jnp.dot(wide_ref[2 * BS:, :], up_ref[...], preferred_element_type=jnp.float32)
    high = jnp.dot(wide_ref[:2 * BS, :], down_ref[...], preferred_element_type=jnp.float32)
    first = core[0] == 0
    own_ref[...] = jnp.where(first, low, high)
    give_ref[...] = jnp.where(first, high, low)


def edge_tiles(core, wide, down, up):
    smem = pl.BlockSpec(memory_space=pltpu.SMEM)
    vmem = pl.BlockSpec(memory_space=pltpu.VMEM)
    out = jax.ShapeDtypeStruct((2 * BS, down.shape[1]), jnp.float32)
    return pl.pallas_call(
        edge_kernel,
        in_specs=[smem, vmem, vmem, vmem],
        out_specs=[vmem, vmem],
        out_shape=[out, out],
        compiler_params=pltpu.CompilerParams(vmem_limit_bytes=32 * 1024 * 1024),
        cost_estimate=pl.CostEstimate(
            flops=800_000_000, bytes_accessed=8_000_000, transcendentals=0
        ),
        name="edge_tiles",
    )(core, wide, down, up)


def cross_kernel(core, flags, own_ref, got_ref, sum_ref, send_ref):
    total = own_ref[...] + got_ref[...]
    upper, lower = total[:BS], total[BS:]
    first = core[0] == 0
    keep_far = flags[4 * 2 + 1] > 0
    keep_near = flags[5 * 2] > 0
    upper = jnp.where(first | keep_far, upper, 0.0)
    lower = jnp.where(first | keep_near, lower, 0.0)
    sum_ref[:BS] = upper
    sum_ref[BS:] = lower
    send_ref[:HALF] = jnp.where(first, lower, upper).T
    near = jnp.where(keep_near, 1.0, 0.0)
    far = jnp.where(flags[5 * 2 + 1] > 0, 1.0, 0.0)
    row = lax.broadcasted_iota(jnp.int32, (8, BS), 0)
    send_ref[HALF:] = jnp.where(row == 0, near, far)


def cross_sums(core, flags, own, got):
    smem = pl.BlockSpec(memory_space=pltpu.SMEM)
    vmem = pl.BlockSpec(memory_space=pltpu.VMEM)
    return pl.pallas_call(
        cross_kernel,
        in_specs=[smem, smem, vmem, vmem],
        out_specs=[vmem, vmem],
        out_shape=[
            jax.ShapeDtypeStruct((2 * BS, HALF), jnp.float32),
            jax.ShapeDtypeStruct((HALF + 8, BS), jnp.float32),
        ],
        name="cross_sums",
    )(core, flags, own, got)


UPPER_SLOTS = (((0, 1, 2), (3, 4, 6), (5, 7, 8)), ((3, 4, 5), (6, 7, -1), (8, -1, -1)))
LOWER_SLOTS = (((-1, -1), (1, -1), (4, 2)), ((1, 0), (4, 2), (7, 5)))


def band_kernel(core, flags, keep_ref, got_ref, upper_ref, lower_ref):
    for which in range(2):

        @pl.when(core[0] == which)
        def _():
            for row in range(3):
                block = 3 * which + row
                for k, slot in enumerate(UPPER_SLOTS[which][row]):
                    if slot >= 0:
                        tile = keep_ref[slot] + got_ref[slot]
                        if k > 0:
                            tile = jnp.where(flags[block * 2 + k - 1] > 0, tile, 0.0)
                        upper_ref[row * BS:(row + 1) * BS, k * BS:(k + 1) * BS] = tile
                for k, slot in enumerate(LOWER_SLOTS[which][row], 1):
                    if slot >= 0:
                        tile = keep_ref[slot] + got_ref[slot]
                        tile = jnp.where(flags[(block - k) * 2 + k - 1] > 0, tile, 0.0)
                        lower_ref[row * BS:(row + 1) * BS, (k - 1) * BS:k * BS] = tile.T


def local_bands(core, flags, keep, got):
    smem = pl.BlockSpec(memory_space=pltpu.SMEM)
    vmem = pl.BlockSpec(memory_space=pltpu.VMEM)
    return pl.pallas_call(
        band_kernel,
        in_specs=[smem, smem, vmem, vmem],
        out_specs=[vmem, vmem],
        out_shape=[
            jax.ShapeDtypeStruct((3 * BS, 3 * BS), jnp.float32),
            jax.ShapeDtypeStruct((3 * BS, 2 * BS), jnp.float32),
        ],
        compiler_params=pltpu.CompilerParams(vmem_limit_bytes=32 * 1024 * 1024),
        cost_estimate=pl.CostEstimate(
            flops=10_000_000, bytes_accessed=10_000_000, transcendentals=0
        ),
        name="local_bands",
    )(core, flags, keep, got)


def finish_kernel(core, flags, *refs):
    sums, crossed = refs[0:2], refs[2:4]
    upper_ref, lower_ref = refs[6:8]
    first_stage, second_stage, third_stage, sems = refs[8:]
    first = core[0] == 0
    for part in range(2):
        cols = pl.ds(part * HALF, HALF)
        keep_near = jnp.where(first, crossed[part][HALF:HALF + 1, :], 1.0)
        keep_far = jnp.where(first, crossed[part][HALF + 1:HALF + 2, :], 1.0)
        first_stage[:, cols] = jnp.where(keep_near[:, :HALF] > 0, sums[part][:BS], 0.0)
        second_stage[:, cols] = jnp.where(keep_far[:, :HALF] > 0, sums[part][BS:], 0.0)
        third = crossed[part][:HALF, :]
        third_stage[pl.ds(part * HALF, HALF), :] = jnp.where(
            first | (flags[5 * 2 + 1] > 0), third, 0.0
        )

    def copies(targets):
        moves = [
            pltpu.make_async_copy(source, target, sems.at[i])
            for i, (source, target) in enumerate(
                zip((first_stage, second_stage, third_stage), targets)
            )
        ]
        for move in moves:
            move.start()
        for move in moves:
            move.wait()

    @pl.when(first)
    def _():
        copies((
            lower_ref.at[pl.ds(0, BS), pl.ds(0, BS)],
            lower_ref.at[pl.ds(BS, BS), pl.ds(BS, BS)],
            lower_ref.at[pl.ds(0, BS), pl.ds(BS, BS)],
        ))

    @pl.when(core[0] == 1)
    def _():
        copies((
            upper_ref.at[pl.ds(BS, BS), pl.ds(2 * BS, BS)],
            upper_ref.at[pl.ds(2 * BS, BS), pl.ds(BS, BS)],
            upper_ref.at[pl.ds(2 * BS, BS), pl.ds(2 * BS, BS)],
        ))


def finish(core, flags, sums, crossed, upper, lower):
    smem = pl.BlockSpec(memory_space=pltpu.SMEM)
    vmem = pl.BlockSpec(memory_space=pltpu.VMEM)
    any_space = pl.BlockSpec(memory_space=pl.ANY)
    return pl.pallas_call(
        finish_kernel,
        in_specs=[smem, smem, vmem, vmem, vmem, vmem, any_space, any_space],
        out_specs=[any_space, any_space],
        out_shape=[
            jax.ShapeDtypeStruct(upper.shape, upper.dtype),
            jax.ShapeDtypeStruct(lower.shape, lower.dtype),
        ],
        input_output_aliases={6: 0, 7: 1},
        scratch_shapes=[pltpu.VMEM((BS, BS), jnp.float32)] * 3
        + [pltpu.SemaphoreType.DMA((3,))],
        name="finish",
    )(core, flags, *sums, *crossed, upper, lower)


def body(factors, pair_keep):
    chips = lax.axis_size("ao")
    axes = ("ao", "aux")
    upward = [(2 * c + k, 2 * c + 2 + k) for c in range(chips - 1) for k in range(2)]
    downward = [(b, a) for a, b in upward]
    swap = [(2 * c + k, 2 * c + 1 - k) for c in range(chips) for k in range(2)]
    cross = [(2 * c + 1, 2 * c + 2) for c in range(chips - 1)]
    cross = cross + [(b, a) for a, b in cross]

    core = lax.axis_index("aux").astype(jnp.int32)
    core_ref = core.reshape(1)
    flags = pair_keep.reshape(-1)
    g = jnp.swapaxes(factors[0], 0, 1)
    top = (BLOCKS - 1) * BS
    downs, ups = [], []
    for part in range(2):
        at = part * HALF
        downs.append(lax.ppermute(g[:, at:at + HALF], axes, downward))
        ups.append(lax.ppermute(g[:, top + at:top + at + HALF], axes, upward))

    keep, give, wide = local_tiles(core, g)
    got = lax.ppermute(give, axes, swap)
    sums, crossed = [], []
    for part in range(2):
        own, other = edge_tiles(core_ref, wide, downs[part], ups[part])
        arrived = lax.ppermute(other, axes, swap)
        total, send = cross_sums(core_ref, flags, own, arrived)
        sums.append(total)
        crossed.append(lax.ppermute(send, axes, cross))
    upper, lower = local_bands(core_ref, flags, keep, got)
    return tuple(finish(core_ref, flags, sums, crossed, upper, lower))


def solution(mesh):
    in_specs = (P("aux", "ao", None), P("ao", None))
    out_specs = (P(("ao", "aux"), None), P(("ao", "aux"), None))
    return jax.shard_map(body, mesh=mesh, in_specs=in_specs, out_specs=out_specs, check_vma=False)
```

time: 168 us -> 98.3 us (0.59); the launches traced: 166 us -> 97.8 us
  Pallas kernels: 0 us -> 31.2 us
  waiting for transfers between devices: 53.2 us -> 22.3 us
  matrix products: 29.8 us -> 0 us
  local copies, waits for them, and re-layouts: 39 us -> 10.5 us
  between operations: 22.1 us -> 0.76 us
  starting transfers between devices: 14.8 us -> 33.1 us
  other arithmetic: 6.53 us -> 0 us
    pallas_call x0 -> x7, Pallas kernels: none -> 31.2 us  [the longest x1 17.8 us: local_tiles(): pl.pallas_call(local_kernel, grid_spec=pltpu.PrefetchScalarGridSpec(num_s...]
    ppermute x2 -> x9, waiting for transfers between devices: 43 us -> 22.3 us  [the longest x2 15.6 us: body(): ups.append(lax.ppermute(g[:, top + at:top + at + HALF], axes, upward))]
    dot_general x6 -> x0, matrix products: 18.5 us -> none  [pair_tile(): jnp.einsum('pai,pbi->ab', operands[0], operands[1], preferred_element_typ...]
    ppermute x2 -> x9, starting transfers between devices: 14.7 us -> 33.1 us  [the longest x2 17.1 us: body(): downs.append(lax.ppermute(g[:, at:at + HALF], axes, downward))]
    unnamed x60 -> x19, local copies, waits for them, and re-layouts: 23.3 us -> 6.98 us
    cond x5 -> x0, matrix products: 11.4 us -> none  [masked_tile(): return lax.cond(flag, pair_tile, empty_tile, (left, right))]
    reduce_scatter x2 -> x0, waiting for transfers between devices: 10.2 us -> none  [the longest x1 10.1 us: body(): lax.psum_scatter(lower_local, 'aux', scatter_dimension=0, tiled=True)]
    squeeze x3 -> x0, local copies, waits for them, and re-layouts: 9.18 us -> none  [the longest x1 6.5 us: body(): own[:, block + offset]]
  transfers between devices with their start and end apart: 4 -> 9, of which waited for: 3 -> 5; matrix products, arithmetic and copies ran while one was open for 25% -> 3% of each run, Pallas kernels for 0% -> 12%
where the time goes in v1:
time: 98.3 us; the launch traced here: 97.8 us
  starting transfers between devices  33.1 us (34%)
  Pallas kernels  31.2 us (32%)
  waiting for transfers between devices  22.3 us (23%)
  local copies, waits for them, and re-layouts  10.5 us (11%)
    pallas_call x1, Pallas kernels, local_tiles(): pl.pallas_call(local_kernel, grid_spec=pltpu.PrefetchScalarGridSpec(num_s...  17.8 us
    ppermute x2, starting transfers between devices, body(): downs.append(lax.ppermute(g[:, at:at + HALF], axes, downward))  17.1 us
    ppermute x2, waiting for transfers between devices, body(): ups.append(lax.ppermute(g[:, top + at:top + at + HALF], axes, upward))  15.6 us
    ppermute x2, starting transfers between devices, body(): crossed.append(lax.ppermute(send, axes, cross))  10.6 us
    unnamed x19, local copies, waits for them, and re-layouts  6.98 us
    ppermute x2, starting transfers between devices, body(): ups.append(lax.ppermute(g[:, top + at:top + at + HALF], axes, upward))  5.41 us
    ppermute x2, waiting for transfers between devices, body(): crossed.append(lax.ppermute(send, axes, cross))  4.12 us
    pallas_call x1, Pallas kernels, local_bands(): pl.pallas_call(band_kernel, in_specs=[smem, smem, vmem, vmem], out_specs=...  4.08 us
  transfers between devices with their start and end apart: 9, of which 5 were waited for; matrix products, arithmetic and copies ran while one was open for 3% of the time, Pallas kernels for 12%

profile of v1, /device:TPU:6, one launch (start us, length us, event | category | flops | bytes accessed | tf_op | source)
XLA Modules:
  0.0 97.8 jit_solution(18179526747331048037)
XLA Ops:
  0.6 0.7 constant_dynamic-slice_fusion
  1.4 17.8 %local_tiles.1 = (f32[9,256,256]{2,1,0:T(8,128)S(1)}, f32[9,256,256]{2,1,0:T(8,128)}, bf16[1024,3000]{1,0:T(8,128)(2,1)}) custom-call(s32[36]{0:T(128)S(1)} %reshape_squeeze.3.table, bf16[3000,1536]{1,0:T(8,128)(2,1)} %bitcast.4), custom_call_target="tpu_custom_call" | custom-call | flops 7000000000 | bytes 20000000 | tf_op jit(solution)/shard_map/local_tiles/pallas_call | solution.py:60
  19.2 2.1 %fusion = (bf16[3000,128]{1,0:T(8,128)(2,1)S(1)}, bf16[3000,128]{1,0:T(8,128)(2,1)S(1)}, bf16[3000,128]{1,0:T(8,128)(2,1)S(1)}, bf16[3000,128]{1,0:T(8,128)(2,1)S(1)}) fusion(bf16[3000,1536]{1,0:T(8,128)(2,1)} %bitcast.5), kind=kLoop, calls=%fused_computation.1 | loop fusion | bytes 6144000 | tf_op jit(solution)/shard_map/slice | solution.py:268
  21.3 3.5 %collective-permute-start.4 = (bf16[3000,128]{1,0:T(8,128)(2,1)S(1)}, bf16[3000,128]{1,0:T(8,128)(2,1)S(1)}, u32[]{:S(2)}, u32[]{:S(2)}) collective-permute-start(bf16[3000,128]{1,0:T(8,128)(2,1)S(1)} %get-tuple-element.28), channel_id=1, source_target_pairs={{0,2},{1,3},{2,4},{3,5},{4,6},{5,7},{6,8},{7,9},{8,10},{9,11},{10,... | collective-permute-start | bytes 2304008 | tf_op jit(solution)/shard_map/ppermute | solution.py:268
  24.8 8.9 %collective-permute-start.3 = (bf16[3000,128]{1,0:T(8,128)(2,1)S(1)}, bf16[3000,128]{1,0:T(8,128)(2,1)S(1)}, u32[]{:S(2)}, u32[]{:S(2)}) collective-permute-start(bf16[3000,128]{1,0:T(8,128)(2,1)S(1)} %get-tuple-element.29), channel_id=1, source_target_pairs={{2,0},{3,1},{4,2},{5,3},{6,4},{7,5},{8,6},{9,7},{10,8},{11,9},{12,... | collective-permute-start | bytes 2304008 | tf_op jit(solution)/shard_map/ppermute | solution.py:267
  33.7 1.9 %collective-permute-start.1 = (bf16[3000,128]{1,0:T(8,128)(2,1)S(1)}, bf16[3000,128]{1,0:T(8,128)(2,1)S(1)}, u32[]{:S(2)}, u32[]{:S(2)}) collective-permute-start(bf16[3000,128]{1,0:T(8,128)(2,1)S(1)} %get-tuple-element.30), channel_id=1, source_target_pairs={{0,2},{1,3},{2,4},{3,5},{4,6},{5,7},{6,8},{7,9},{8,10},{9,11},{10,... | collective-permute-start | bytes 2304008 | tf_op jit(solution)/shard_map/ppermute | solution.py:268
  35.6 8.1 %collective-permute-start = (bf16[3000,128]{1,0:T(8,128)(2,1)S(1)}, bf16[3000,128]{1,0:T(8,128)(2,1)S(1)}, u32[]{:S(2)}, u32[]{:S(2)}) collective-permute-start(bf16[3000,128]{1,0:T(8,128)(2,1)S(1)} %get-tuple-element.31), channel_id=1, source_target_pairs={{2,0},{3,1},{4,2},{5,3},{6,4},{7,5},{8,6},{9,7},{10,8},{11,9},{12,... | collective-permute-start | bytes 2304008 | tf_op jit(solution)/shard_map/ppermute | solution.py:267
  43.8 6.0 %collective-permute-done.4.up_ref = bf16[3000,128]{1,0:T(8,128)(2,1)S(1)} collective-permute-done((bf16[3000,128]{1,0:T(8,128)(2,1)S(1)}, bf16[3000,128]{1,0:T(8,128)(2,1)S(1)}, u32[]{:S(2)}, u32[]{:S(2)}) %collective-permute-start.4) | collective-permute-done | bytes 768032 | tf_op jit(solution)/shard_map/ppermute | solution.py:268
  49.7 1.4 %collective-permute-done.3.down_ref = bf16[3000,128]{1,0:T(8,128)(2,1)S(1)} collective-permute-done((bf16[3000,128]{1,0:T(8,128)(2,1)S(1)}, bf16[3000,128]{1,0:T(8,128)(2,1)S(1)}, u32[]{:S(2)}, u32[]{:S(2)}) %collective-permute-start.3) | collective-permute-done | bytes 768032 | tf_op jit(solution)/shard_map/ppermute | solution.py:267
  51.1 2.8 %copy-done = bf16[1024,3000]{1,0:T(8,128)(2,1)S(1)} copy-done((bf16[1024,3000]{1,0:T(8,128)(2,1)S(1)}, bf16[1024,3000]{1,0:T(8,128)(2,1)}, u32[]{:S(2)}) %copy-start) | copy-done | bytes 6144024
  53.9 1.8 %edge_tiles.3 = (f32[512,128]{1,0:T(8,128)S(1)}, f32[512,128]{1,0:T(8,128)S(1)}) custom-call(s32[1]{0:T(128)} %bitcast.core, bf16[1024,3000]{1,0:T(8,128)(2,1)S(1)} %copy-done, bf16[3000,128]{1,0:T(8,128)(2,1)S(1)} %collective-permute-done.3.down_ref, bf16[3000,128]{1,0:T(8,128)(2,1)S(1)} %collective-permute-done.4.up_ref), custom_call_target="tpu_custom_call" | custom-call | flops 800000000 | bytes 8000000 | tf_op jit(solution)/shard_map/edge_tiles/pallas_call | solution.py:98
  55.7 0.7 copy-done.1
  56.4 9.6 %collective-permute-done.1.up_ref = bf16[3000,128]{1,0:T(8,128)(2,1)S(1)} collective-permute-done((bf16[3000,128]{1,0:T(8,128)(2,1)S(1)}, bf16[3000,128]{1,0:T(8,128)(2,1)S(1)}, u32[]{:S(2)}, u32[]{:S(2)}) %collective-permute-start.1) | collective-permute-done | bytes 768032 | tf_op jit(solution)/shard_map/ppermute | solution.py:268
  66.0 1.2 %collective-permute-done.down_ref = bf16[3000,128]{1,0:T(8,128)(2,1)S(1)} collective-permute-done((bf16[3000,128]{1,0:T(8,128)(2,1)S(1)}, bf16[3000,128]{1,0:T(8,128)(2,1)S(1)}, u32[]{:S(2)}, u32[]{:S(2)}) %collective-permute-start) | collective-permute-done | bytes 768032 | tf_op jit(solution)/shard_map/ppermute | solution.py:267
  67.2 1.8 %edge_tiles.2 = (f32[512,128]{1,0:T(8,128)S(1)}, f32[512,128]{1,0:T(8,128)S(1)}) custom-call(s32[1]{0:T(128)} %bitcast.core, bf16[1024,3000]{1,0:T(8,128)(2,1)S(1)} %copy-done, bf16[3000,128]{1,0:T(8,128)(2,1)S(1)} %collective-permute-done.down_ref, bf16[3000,128]{1,0:T(8,128)(2,1)S(1)} %collective-permute-done.1.up_ref), custom_call_target="tpu_custom_call" | custom-call | flops 800000000 | bytes 8000000 | tf_op jit(solution)/shard_map/edge_tiles/pallas_call | solution.py:98
  69.0 0.7 copy-done.2
  70.5 0.7 copy-done.4
  71.2 1.8 %cross_sums.3 = (f32[512,128]{1,0:T(8,128)}, f32[136,256]{1,0:T(8,128)}) custom-call(s32[1]{0:T(128)} %bitcast.core, s32[12]{0:T(128)} %reshape.11.flags, f32[512,128]{1,0:T(8,128)} %copy-done.1, f32[512,128]{1,0:T(8,128)} %copy-done.4), custom_call_target="tpu_custom_call" | custom-call | tf_op jit(solution)/shard_map/cross_sums/pallas_call | solution.py:131
  73.0 8.7 %collective-permute-start.7 = (f32[136,256]{1,0:T(8,128)}, f32[136,256]{1,0:T(8,128)S(1)}, u32[]{:S(2)}, u32[]{:S(2)}) collective-permute-start(f32[136,256]{1,0:T(8,128)} %get-tuple-element.23), channel_id=1, source_target_pairs={{1,2},{3,4},{5,6},{7,8},{9,10},{11,12},{13,14},{15,16},{17,18},{19... | collective-permute-start | bytes 417800 | tf_op jit(solution)/shard_map/ppermute | solution.py:278
  82.4 1.9 %cross_sums.2 = (f32[512,128]{1,0:T(8,128)}, f32[136,256]{1,0:T(8,128)}) custom-call(s32[1]{0:T(128)} %bitcast.core, s32[12]{0:T(128)} %reshape.11.flags, f32[512,128]{1,0:T(8,128)} %copy-done.2, f32[512,128]{1,0:T(8,128)} %copy-done.5), custom_call_target="tpu_custom_call" | custom-call | tf_op jit(solution)/shard_map/cross_sums/pallas_call | solution.py:131
  84.3 1.9 %collective-permute-start.6 = (f32[136,256]{1,0:T(8,128)}, f32[136,256]{1,0:T(8,128)S(1)}, u32[]{:S(2)}, u32[]{:S(2)}) collective-permute-start(f32[136,256]{1,0:T(8,128)} %get-tuple-element.22), channel_id=1, source_target_pairs={{1,2},{3,4},{5,6},{7,8},{9,10},{11,12},{13,14},{15,16},{17,18},{19... | collective-permute-start | bytes 417800 | tf_op jit(solution)/shard_map/ppermute | solution.py:278
  86.9 4.1 %local_bands.1 = (f32[768,768]{1,0:T(8,128)}, f32[768,512]{1,0:T(8,128)}) custom-call(s32[1]{0:T(128)} %bitcast.core, s32[12]{0:T(128)S(1)} %copy-done.3, f32[9,256,256]{2,1,0:T(8,128)S(1)} %get-tuple-element.24.keep_ref, f32[9,256,256]{2,1,0:T(8,128)} %collective-permute-done.8.got_ref), custom_call_target="tpu_custom_call" | custom-call | flops 10000000 | bytes 10000000 | tf_op jit(solution)/shard_map/local_bands/pallas_call | solution.py:170
  91.0 4.1 %collective-permute-done.6.refs_2_ = f32[136,256]{1,0:T(8,128)S(1)} collective-permute-done((f32[136,256]{1,0:T(8,128)}, f32[136,256]{1,0:T(8,128)S(1)}, u32[]{:S(2)}, u32[]{:S(2)}) %collective-permute-start.6) | collective-permute-done | bytes 139296 | tf_op jit(solution)/shard_map/ppermute | solution.py:278
  95.7 2.0 %finish.1 = (f32[768,768]{1,0:T(8,128)}, f32[768,512]{1,0:T(8,128)}) custom-call(s32[1]{0:T(128)} %bitcast.core, s32[12]{0:T(128)} %reshape.11.flags, f32[512,128]{1,0:T(8,128)} %get-tuple-element.18.refs_0_, f32[512,128]{1,0:T(8,128)} %get-tuple-element.21.refs_1_, f32[136,256]{1,0:T(8,128)} %copy-done.7, ...), custom_call_target="tpu_custom_call", output_to_operand_aliasing={{0}: (6, {}), {1}: (7, {})} | custom-call | tf_op jit(solution)/shard_map/finish/pallas_call | solution.py:235
  (24 shorter events, 2.9 us)
Async XLA Ops:
  19.2 67.0 %collective-permute-start.8 = (f32[9,256,256]{2,1,0:T(8,128)}, f32[9,256,256]{2,1,0:T(8,128)}, u32[]{:S(2)}, u32[]{:S(2)}) collective-permute-start(f32[9,256,256]{2,1,0:T(8,128)} %get-tuple-element.25), channel_id=1, source_target_pairs={{0,1},{1,0},{2,3},{3,2},{4,5},{5,4},{6,7},{7,6},{8,9},{9,8},{10,11... | collective-permute-start | bytes 7077896 | tf_op jit(solution)/shard_map/ppermute | solution.py:271
  21.3 28.5 %collective-permute-start.4 = (bf16[3000,128]{1,0:T(8,128)(2,1)S(1)}, bf16[3000,128]{1,0:T(8,128)(2,1)S(1)}, u32[]{:S(2)}, u32[]{:S(2)}) collective-permute-start(bf16[3000,128]{1,0:T(8,128)(2,1)S(1)} %get-tuple-element.28), channel_id=1, source_target_pairs={{0,2},{1,3},{2,4},{3,5},{4,6},{5,7},{6,8},{7,9},{8,10},{9,11},{10,... | collective-permute-start | bytes 2304008 | tf_op jit(solution)/shard_map/ppermute | solution.py:268
  24.8 26.4 %collective-permute-start.3 = (bf16[3000,128]{1,0:T(8,128)(2,1)S(1)}, bf16[3000,128]{1,0:T(8,128)(2,1)S(1)}, u32[]{:S(2)}, u32[]{:S(2)}) collective-permute-start(bf16[3000,128]{1,0:T(8,128)(2,1)S(1)} %get-tuple-element.29), channel_id=1, source_target_pairs={{2,0},{3,1},{4,2},{5,3},{6,4},{7,5},{8,6},{9,7},{10,8},{11,9},{12,... | collective-permute-start | bytes 2304008 | tf_op jit(solution)/shard_map/ppermute | solution.py:267
  33.7 32.3 %collective-permute-start.1 = (bf16[3000,128]{1,0:T(8,128)(2,1)S(1)}, bf16[3000,128]{1,0:T(8,128)(2,1)S(1)}, u32[]{:S(2)}, u32[]{:S(2)}) collective-permute-start(bf16[3000,128]{1,0:T(8,128)(2,1)S(1)} %get-tuple-element.30), channel_id=1, source_target_pairs={{0,2},{1,3},{2,4},{3,5},{4,6},{5,7},{6,8},{7,9},{8,10},{9,11},{10,... | collective-permute-start | bytes 2304008 | tf_op jit(solution)/shard_map/ppermute | solution.py:268
  35.6 31.6 %collective-permute-start = (bf16[3000,128]{1,0:T(8,128)(2,1)S(1)}, bf16[3000,128]{1,0:T(8,128)(2,1)S(1)}, u32[]{:S(2)}, u32[]{:S(2)}) collective-permute-start(bf16[3000,128]{1,0:T(8,128)(2,1)S(1)} %get-tuple-element.31), channel_id=1, source_target_pairs={{2,0},{3,1},{4,2},{5,3},{6,4},{7,5},{8,6},{9,7},{10,8},{11,9},{12,... | collective-permute-start | bytes 2304008 | tf_op jit(solution)/shard_map/ppermute | solution.py:267
  51.1 2.8 %copy-start = (bf16[1024,3000]{1,0:T(8,128)(2,1)S(1)}, bf16[1024,3000]{1,0:T(8,128)(2,1)}, u32[]{:S(2)}) copy-start(bf16[1024,3000]{1,0:T(8,128)(2,1)} %get-tuple-element.15.wide_ref) | copy-start | bytes 18432004
  55.7 0.7 copy-start.1
  56.4 13.3 %copy-start.8 = (s32[6,2]{0,1:T(2,128)S(1)}, s32[6,2]{0,1:T(2,128)}, u32[]{:S(2)}) copy-start(s32[6,2]{0,1:T(2,128)} %param.4) | copy-start | bytes 148
  56.4 14.0 %collective-permute-start.5 = (f32[512,128]{1,0:T(8,128)S(1)}, f32[512,128]{1,0:T(8,128)S(1)}, u32[]{:S(2)}, u32[]{:S(2)}) collective-permute-start(f32[512,128]{1,0:T(8,128)S(1)} %get-tuple-element.20), channel_id=1, source_target_pairs={{0,1},{1,0},{2,3},{3,2},{4,5},{5,4},{6,7},{7,6},{8,9},{9,8},{10,11... | collective-permute-start | bytes 786440 | tf_op jit(solution)/shard_map/ppermute | solution.py:275
  69.0 0.7 copy-start.2
  69.7 12.0 %collective-permute-start.2 = (f32[512,128]{1,0:T(8,128)S(1)}, f32[512,128]{1,0:T(8,128)S(1)}, u32[]{:S(2)}, u32[]{:S(2)}) collective-permute-start(f32[512,128]{1,0:T(8,128)S(1)} %get-tuple-element.17), channel_id=1, source_target_pairs={{0,1},{1,0},{2,3},{3,2},{4,5},{5,4},{6,7},{7,6},{8,9},{9,8},{10,11... | collective-permute-start | bytes 786440 | tf_op jit(solution)/shard_map/ppermute | solution.py:275
  70.5 0.7 copy-start.4
  73.0 18.0 %collective-permute-start.7 = (f32[136,256]{1,0:T(8,128)}, f32[136,256]{1,0:T(8,128)S(1)}, u32[]{:S(2)}, u32[]{:S(2)}) collective-permute-start(f32[136,256]{1,0:T(8,128)} %get-tuple-element.23), channel_id=1, source_target_pairs={{1,2},{3,4},{5,6},{7,8},{9,10},{11,12},{13,14},{15,16},{17,18},{19... | collective-permute-start | bytes 417800 | tf_op jit(solution)/shard_map/ppermute | solution.py:278
  81.7 0.7 copy-start.5
  84.3 10.8 %collective-permute-start.6 = (f32[136,256]{1,0:T(8,128)}, f32[136,256]{1,0:T(8,128)S(1)}, u32[]{:S(2)}, u32[]{:S(2)}) collective-permute-start(f32[136,256]{1,0:T(8,128)} %get-tuple-element.22), channel_id=1, source_target_pairs={{1,2},{3,4},{5,6},{7,8},{9,10},{11,12},{13,14},{15,16},{17,18},{19... | collective-permute-start | bytes 417800 | tf_op jit(solution)/shard_map/ppermute | solution.py:278
  86.2 0.7 copy-start.3
  91.0 4.1 %copy-start.6 = (f32[136,256]{1,0:T(8,128)}, f32[136,256]{1,0:T(8,128)S(1)}, u32[]{:S(2)}) copy-start(f32[136,256]{1,0:T(8,128)S(1)} %collective-permute-done.7.refs_3_) | copy-start | bytes 417796
  95.1 0.7 copy-start.7

commit v2 on v0

v2 whole, which is shorter than its diff:
```python
import jax
import jax.numpy as jnp
from jax import lax
from jax.experimental import pallas as pl
from jax.experimental.pallas import tpu as pltpu
from jax.sharding import PartitionSpec as P

BS = 256
BLOCKS = 6
HELD = 3
SLOTS = HELD * HELD
MIB = 1024 * 1024

BORROWED = {(1, 2): 7, (2, 1): 5, (2, 2): 8}
UPPER = (((0, 1, 2), (3, 4, 5), (6, 7, 8)), ((0, 1, 2), (3, 4, -1), (6, -1, -1)))
LOWER = (((-1, -1), (1, -1), (4, 2)), ((5, 7), (1, 8), (4, 2)))

SMEM = pl.BlockSpec(memory_space=pltpu.SMEM)
VMEM = pl.BlockSpec(memory_space=pltpu.VMEM)
ANY = pl.BlockSpec(memory_space=pl.ANY)
OVER_ROWS = (((0,), (0,)), ((), ()))


def cut_kernel(g_ref, one_ref, two_ref, sems):
    core = lax.axis_index("aux")
    last = (BLOCKS - 1) * BS
    moves = [
        pltpu.make_async_copy(
            g_ref.at[:, pl.ds(pl.multiple_of(start, BS), BS)], out, sems.at[i]
        )
        for i, (start, out) in enumerate(((core * last, one_ref), ((1 - core) * last, two_ref)))
    ]
    for move in moves:
        move.start()
    for move in moves:
        move.wait()


def cut(g):
    out = jax.ShapeDtypeStruct((g.shape[0], BS), g.dtype)
    return pl.pallas_call(
        cut_kernel,
        in_specs=[ANY],
        out_specs=[ANY, ANY],
        out_shape=[out, out],
        scratch_shapes=[pltpu.SemaphoreType.DMA((2,))],
        compiler_params=pltpu.CompilerParams(vmem_limit_bytes=52 * MIB),
        cost_estimate=pl.CostEstimate(flops=0, bytes_accessed=3_000_000, transcendentals=0),
        name="cut",
    )(g)


def local_kernel(flags, g_ref, keep_ref, give_ref, mask_ref, held, sems):
    core = lax.axis_index("aux")
    loads = []
    for block in range(BLOCKS):
        cols = pl.ds(block * BS, BS)
        loads.append(pltpu.make_async_copy(g_ref.at[:, cols], held.at[:, cols], sems.at[block]))
    for load in reversed(loads):
        load.start()

    row = lax.broadcasted_iota(jnp.int32, (8, BS), 0)
    near, far, other = flags[0, BLOCKS - 1], flags[1, BLOCKS - 1], flags[1, BLOCKS - 2]
    values = jnp.where(row == 0, near, jnp.where(row == 1, far, other))
    mask_ref[...] = values.astype(jnp.float32)

    def row_of_tiles(m, count):
        left = held[:, pl.ds(pl.multiple_of(m * BS, BS), BS)]
        right = held[:, pl.ds(pl.multiple_of(m * BS, BS), count * BS)]
        tiles = lax.dot_general(left, right, OVER_ROWS, preferred_element_type=jnp.float32)
        owner = m // HELD
        for k in range(count):
            tile = tiles[:, k * BS:(k + 1) * BS]
            if k > 0:
                tile = jnp.where(flags[k - 1, m] > 0, tile, 0.0)
            slot = HELD * (m - HELD * owner) + k

            @pl.when(owner == core)
            def _():
                keep_ref[slot] = tile

            @pl.when(owner != core)
            def _():
                give_ref[slot] = tile

            for (row, offset), borrowed in BORROWED.items():
                if offset == k:

                    @pl.when((m == row) & (core == 1))
                    def _():
                        keep_ref[borrowed] = tile

                    @pl.when((m == row) & (core == 0))
                    def _():
                        give_ref[borrowed] = tile

    for count in (1, 2):
        loads[BLOCKS - count].wait()
        row_of_tiles(jnp.int32(BLOCKS - count), count)

    def step(i, carry):
        m = BLOCKS - 3 - i
        cols = pl.ds(pl.multiple_of(m * BS, BS), BS)
        pltpu.make_async_copy(g_ref.at[:, cols], held.at[:, cols], sems.at[m]).wait()
        row_of_tiles(m, 3)
        return carry

    lax.fori_loop(0, BLOCKS - 2, step, 0)


def local_tiles(flags, g):
    nocc = g.shape[0]
    return pl.pallas_call(
        local_kernel,
        in_specs=[SMEM, ANY],
        out_specs=[VMEM, VMEM, VMEM],
        out_shape=[
            jax.ShapeDtypeStruct((SLOTS, BS, BS), jnp.float32),
            jax.ShapeDtypeStruct((SLOTS, BS, BS), jnp.float32),
            jax.ShapeDtypeStruct((8, BS), jnp.float32),
        ],
        scratch_shapes=[
            pltpu.VMEM((nocc, BLOCKS * BS), jnp.bfloat16),
            pltpu.SemaphoreType.DMA((BLOCKS,)),
        ],
        compiler_params=pltpu.CompilerParams(vmem_limit_bytes=44 * MIB),
        cost_estimate=pl.CostEstimate(
            flops=12_000_000_000, bytes_accessed=20_000_000, transcendentals=0
        ),
        name="local_tiles",
    )(flags, g)


def edge_kernel(g_ref, came_ref, give_ref, turned_ref, one, two, sems):
    core = lax.axis_index("aux")
    far = (BLOCKS - 2) * BS
    loads = []
    for i, (start, held) in enumerate((((1 - core) * far, one), (core * far, two))):
        cols = pl.ds(pl.multiple_of(start, BS), 2 * BS)
        loads.append(pltpu.make_async_copy(g_ref.at[:, cols], held, sems.at[i]))
    for load in loads:
        load.start()
    loads[0].wait()
    give_ref[...] = lax.dot_general(
        one[...], came_ref[...], OVER_ROWS, preferred_element_type=jnp.float32
    )
    loads[1].wait()
    turned_ref[...] = two[...].T


def edge_partial(g, came):
    nocc = g.shape[0]
    return pl.pallas_call(
        edge_kernel,
        in_specs=[ANY, VMEM],
        out_specs=[VMEM, VMEM],
        out_shape=[
            jax.ShapeDtypeStruct((2 * BS, BS), jnp.float32),
            jax.ShapeDtypeStruct((2 * BS, nocc), jnp.bfloat16),
        ],
        scratch_shapes=[pltpu.VMEM((nocc, 2 * BS), jnp.bfloat16)] * 2
        + [pltpu.SemaphoreType.DMA((2,))],
        compiler_params=pltpu.CompilerParams(vmem_limit_bytes=44 * MIB),
        cost_estimate=pl.CostEstimate(
            flops=1_600_000_000, bytes_accessed=8_000_000, transcendentals=0
        ),
        name="edge_partial",
    )(g, came)


def band_kernel(keep_ref, got_ref, upper_ref, lower_ref):
    core = lax.axis_index("aux")
    for which in range(2):

        @pl.when(core == which)
        def _():
            for row in range(HELD):
                for k, slot in enumerate(UPPER[which][row]):
                    if slot >= 0:
                        tile = keep_ref[slot] + got_ref[slot]
                        upper_ref[row * BS:(row + 1) * BS, k * BS:(k + 1) * BS] = tile
                for k, slot in enumerate(LOWER[which][row]):
                    if slot >= 0:
                        tile = keep_ref[slot] + got_ref[slot]
                        lower_ref[row * BS:(row + 1) * BS, k * BS:(k + 1) * BS] = tile.T


def local_bands(keep, got):
    return pl.pallas_call(
        band_kernel,
        in_specs=[VMEM, VMEM],
        out_specs=[VMEM, VMEM],
        out_shape=[
            jax.ShapeDtypeStruct((HELD * BS, 3 * BS), jnp.float32),
            jax.ShapeDtypeStruct((HELD * BS, 2 * BS), jnp.float32),
        ],
        compiler_params=pltpu.CompilerParams(vmem_limit_bytes=24 * MIB),
        cost_estimate=pl.CostEstimate(
            flops=10_000_000, bytes_accessed=12_000_000, transcendentals=0
        ),
        name="local_bands",
    )(keep, got)


def sum_kernel(turned_ref, came_ref, got_ref, mask_ref, sum_ref, send_ref):
    total = jnp.dot(turned_ref[...], came_ref[...], preferred_element_type=jnp.float32)
    first = lax.axis_index("aux") == 0
    near = jnp.where(first, 1.0, mask_ref[0:1, :])
    other_pair = jnp.where(first, 1.0, mask_ref[2:3, :])
    top = jnp.where(other_pair > 0, total[:BS] + got_ref[:BS], 0.0)
    low = jnp.where(near > 0, total[BS:] + got_ref[BS:], 0.0)
    sum_ref[:BS] = top
    sum_ref[BS:] = low
    send_ref[:BS] = jnp.where(first, low, top).T
    send_ref[BS:] = mask_ref[...]


def edge_sum(turned, came, got, mask):
    return pl.pallas_call(
        sum_kernel,
        in_specs=[VMEM] * 4,
        out_specs=[VMEM, VMEM],
        out_shape=[
            jax.ShapeDtypeStruct((2 * BS, BS), jnp.float32),
            jax.ShapeDtypeStruct((BS + 8, BS), jnp.float32),
        ],
        compiler_params=pltpu.CompilerParams(vmem_limit_bytes=16 * MIB),
        cost_estimate=pl.CostEstimate(
            flops=1_600_000_000, bytes_accessed=5_000_000, transcendentals=0
        ),
        name="edge_sum",
    )(turned, came, got, mask)


def finish_kernel(sum_ref, cross_ref, mask_ref, _, __, upper_ref, lower_ref, *scratch):
    stages, sems = scratch[:3], scratch[3]
    core = lax.axis_index("aux")
    first = core == 0
    near = jnp.where(first, cross_ref[BS:BS + 1, :], 1.0)
    far = jnp.where(first, cross_ref[BS + 1:BS + 2, :], 1.0)
    third = jnp.where(first, 1.0, mask_ref[1:2, :])
    stages[0][...] = jnp.where(near > 0, sum_ref[:BS], 0.0)
    stages[1][...] = jnp.where(far > 0, sum_ref[BS:], 0.0)
    stages[2][...] = jnp.where(third > 0, cross_ref[:BS], 0.0)

    def copies(band, places):
        moves = [
            pltpu.make_async_copy(
                stage, band.at[pl.ds(row * BS, BS), pl.ds(col * BS, BS)], sems.at[i]
            )
            for i, (stage, (row, col)) in enumerate(zip(stages, places))
        ]
        for move in moves:
            move.start()
        for move in moves:
            move.wait()

    @pl.when(first)
    def _():
        copies(lower_ref, ((0, 0), (1, 1), (0, 1)))

    @pl.when(core == 1)
    def _():
        copies(upper_ref, ((1, 2), (2, 1), (2, 2)))


def finish(total, crossed, mask, upper, lower):
    return pl.pallas_call(
        finish_kernel,
        in_specs=[VMEM, VMEM, VMEM, ANY, ANY],
        out_specs=[ANY, ANY],
        out_shape=[
            jax.ShapeDtypeStruct(upper.shape, upper.dtype),
            jax.ShapeDtypeStruct(lower.shape, lower.dtype),
        ],
        input_output_aliases={3: 0, 4: 1},
        scratch_shapes=[pltpu.VMEM((BS, BS), jnp.float32)] * 3
        + [pltpu.SemaphoreType.DMA((3,))],
        name="finish",
    )(total, crossed, mask, upper, lower)


def body(factors, pair_keep):
    chips = lax.axis_size("ao")
    axes = ("ao", "aux")
    edges = [(c, c + 1) for c in range(chips - 1)]
    leg_one = [(2 * b, 2 * a) for a, b in edges] + [(2 * a + 1, 2 * b + 1) for a, b in edges]
    leg_two = [(2 * a, 2 * b) for a, b in edges] + [(2 * b + 1, 2 * a + 1) for a, b in edges]
    swap = [(2 * c + k, 2 * c + 1 - k) for c in range(chips) for k in range(2)]
    ahead = [(2 * a + 1, 2 * b) for a, b in edges]
    cross = ahead + [(b, a) for a, b in ahead]

    g = jnp.swapaxes(factors[0], 0, 1)
    flags = jnp.swapaxes(pair_keep, 0, 1)
    one, two = cut(g)
    came_one = lax.ppermute(one, axes, leg_one)
    came_two = lax.ppermute(two, axes, leg_two)
    edge_give, turned = edge_partial(g, came_one)
    edge_got = lax.ppermute(edge_give, axes, swap)
    keep, give, mask = local_tiles(flags, g)
    got = lax.ppermute(give, axes, swap)
    total, send = edge_sum(turned, came_two, edge_got, mask)
    crossed = lax.ppermute(send, axes, cross)
    upper, lower = local_bands(keep, got)
    return tuple(finish(total, crossed, mask, upper, lower))


def solution(mesh):
    in_specs = (P("aux", "ao", None), P("ao", None))
    out_specs = (P(("ao", "aux"), None), P(("ao", "aux"), None))
    return jax.shard_map(body, mesh=mesh, in_specs=in_specs, out_specs=out_specs, check_vma=False)
```

time: 168 us -> 112 us (0.67); the launches traced: 166 us -> 112 us
  Pallas kernels: 0 us -> 66.9 us
  local copies, waits for them, and re-layouts: 39 us -> 1.51 us
  matrix products: 29.8 us -> 0 us
  waiting for transfers between devices: 53.2 us -> 24.1 us
  between operations: 22.1 us -> 0.76 us
  other arithmetic: 6.53 us -> 0 us
  starting transfers between devices: 14.8 us -> 18.3 us
    pallas_call x0 -> x6, Pallas kernels: none -> 66.9 us  [the longest x1 47.7 us: cut(): pl.pallas_call(cut_kernel, in_specs=[ANY], out_specs=[ANY, ANY], out_shap...]
    unnamed x60 -> x10, local copies, waits for them, and re-layouts: 23.3 us -> 1.51 us
    ppermute x2 -> x5, waiting for transfers between devices: 43 us -> 24.1 us  [the longest x1 10.6 us: body(): came_two = lax.ppermute(two, axes, leg_two)]
    dot_general x6 -> x0, matrix products: 18.5 us -> none  [pair_tile(): jnp.einsum('pai,pbi->ab', operands[0], operands[1], preferred_element_typ...]
    cond x5 -> x0, matrix products: 11.4 us -> none  [masked_tile(): return lax.cond(flag, pair_tile, empty_tile, (left, right))]
    reduce_scatter x2 -> x0, waiting for transfers between devices: 10.2 us -> none  [the longest x1 10.1 us: body(): lax.psum_scatter(lower_local, 'aux', scatter_dimension=0, tiled=True)]
    squeeze x3 -> x0, local copies, waits for them, and re-layouts: 9.18 us -> none  [the longest x1 6.5 us: body(): own[:, block + offset]]
    slice x3 -> x0, local copies, waits for them, and re-layouts: 5.75 us -> none  [the longest x2 5.06 us: body(): edge = from_behind(own[:, :partners], 'ao', -1)]
  transfers between devices with their start and end apart: 4 -> 5, of which waited for: 3 -> 3; matrix products, arithmetic and copies ran while one was open for 25% -> 0% of each run, Pallas kernels for 0% -> 15%
where the time goes in v2:
time: 112 us
  Pallas kernels  66.9 us (60%)
  waiting for transfers between devices  24.1 us (22%)
  starting transfers between devices  18.3 us (16%)
  local copies, waits for them, and re-layouts  1.51 us (1%)
    pallas_call x1, Pallas kernels, cut(): pl.pallas_call(cut_kernel, in_specs=[ANY], out_specs=[ANY, ANY], out_shap...  47.7 us
    ppermute x1, waiting for transfers between devices, body(): came_two = lax.ppermute(two, axes, leg_two)  10.6 us
    ppermute x1, starting transfers between devices, body(): came_one = lax.ppermute(one, axes, leg_one)  10.5 us
    pallas_call x1, Pallas kernels, local_tiles(): pl.pallas_call(local_kernel, in_specs=[SMEM, ANY], out_specs=[VMEM, VMEM,...  9.95 us
    ppermute x1, waiting for transfers between devices, body(): came_one = lax.ppermute(one, axes, leg_one)  9.6 us
    ppermute x1, starting transfers between devices, body(): crossed = lax.ppermute(send, axes, cross)  5.76 us
    pallas_call x1, Pallas kernels, edge_partial(): pl.pallas_call(edge_kernel, in_specs=[ANY, VMEM], out_specs=[VMEM, VMEM],...  3.85 us
    ppermute x1, waiting for transfers between devices, body(): crossed = lax.ppermute(send, axes, cross)  3.84 us
  transfers between devices with their start and end apart: 5, of which 3 were waited for; matrix products, arithmetic and copies ran while one was open for 0% of the time, Pallas kernels for 15%

profile of v2, /device:TPU:6, one launch (start us, length us, event | category | flops | bytes accessed | tf_op | source)
XLA Modules:
  0.0 111.6 jit_solution(7284241547014439938)
XLA Ops:
  0.6 0.0 copy-start.2
  0.6 47.7 %cut.1 = (bf16[3000,256]{1,0:T(8,128)(2,1)S(1)}, bf16[3000,256]{1,0:T(8,128)(2,1)}) custom-call(bf16[3000,1536]{1,0:T(8,128)(2,1)} %bitcast.5), custom_call_target="tpu_custom_call" | custom-call | bytes 3000000 | tf_op jit(solution)/shard_map/cut/pallas_call | solution.py:41
  48.3 10.5 %collective-permute-start = (bf16[3000,256]{1,0:T(8,128)(2,1)S(1)}, bf16[3000,256]{1,0:T(8,128)(2,1)S(1)}, u32[]{:S(2)}, u32[]{:S(2)}) collective-permute-start(bf16[3000,256]{1,0:T(8,128)(2,1)S(1)} %get-tuple-element.13), channel_id=1, source_target_pairs={{2,0},{4,2},{6,4},{8,6},{10,8},{12,10},{14,12},{16,14},{18,16},{20... | collective-permute-start | bytes 4608008 | tf_op jit(solution)/shard_map/ppermute | solution.py:296
  58.8 0.0 copy-done.2
  58.8 0.0 copy-start.4
  58.8 10.0 %local_tiles.1 = (f32[9,256,256]{2,1,0:T(8,128)S(1)}, f32[9,256,256]{2,1,0:T(8,128)S(1)}, f32[8,256]{1,0:T(8,128)S(1)}) custom-call(s32[2,6]{1,0:T(2,128)S(1)} %bitcast.4, bf16[3000,1536]{1,0:T(8,128)(2,1)} %bitcast.6), custom_call_target="tpu_custom_call" | custom-call | flops 12000000000 | bytes 20000000 | tf_op jit(solution)/shard_map/local_tiles/pallas_call | solution.py:113
  68.8 0.0 copy-start.1
  68.8 0.1 collective-permute-start.4
  68.9 0.0 copy-done.4
  68.9 1.9 %collective-permute-start.1 = (bf16[3000,256]{1,0:T(8,128)(2,1)S(1)}, bf16[3000,256]{1,0:T(8,128)(2,1)S(1)}, u32[]{:S(2)}, u32[]{:S(2)}) collective-permute-start(bf16[3000,256]{1,0:T(8,128)(2,1)S(1)} %copy-done.4), channel_id=1, source_target_pairs={{0,2},{2,4},{4,6},{6,8},{8,10},{10,12},{12,14},{14,16},{16,18},{18... | collective-permute-start | bytes 4608008 | tf_op jit(solution)/shard_map/ppermute | solution.py:297
  70.8 9.6 %collective-permute-done.came_ref = bf16[3000,256]{1,0:T(8,128)(2,1)S(1)} collective-permute-done((bf16[3000,256]{1,0:T(8,128)(2,1)S(1)}, bf16[3000,256]{1,0:T(8,128)(2,1)S(1)}, u32[]{:S(2)}, u32[]{:S(2)}) %collective-permute-start) | collective-permute-done | bytes 1536032 | tf_op jit(solution)/shard_map/ppermute | solution.py:296
  80.4 3.9 %edge_partial.1 = (f32[512,256]{1,0:T(8,128)S(1)}, bf16[512,3000]{1,0:T(8,128)(2,1)S(1)}) custom-call(bf16[3000,1536]{1,0:T(8,128)(2,1)} %bitcast.7, bf16[3000,256]{1,0:T(8,128)(2,1)S(1)} %collective-permute-done.came_ref), custom_call_target="tpu_custom_call" | custom-call | flops 1600000000 | bytes 8000000 | tf_op jit(solution)/shard_map/edge_partial/pallas_call | solution.py:153
  84.3 0.1 collective-permute-start.2
  84.4 10.6 %collective-permute-done.1.came_ref = bf16[3000,256]{1,0:T(8,128)(2,1)S(1)} collective-permute-done((bf16[3000,256]{1,0:T(8,128)(2,1)S(1)}, bf16[3000,256]{1,0:T(8,128)(2,1)S(1)}, u32[]{:S(2)}, u32[]{:S(2)}) %collective-permute-start.1) | collective-permute-done | bytes 1536032 | tf_op jit(solution)/shard_map/ppermute | solution.py:297
  95.0 0.0 collective-permute-done.2.got_ref
  95.0 0.0 copy-done.1
  95.0 1.1 edge_sum.1
  96.1 0.8 copy-done
  96.9 5.8 %collective-permute-start.3 = (f32[264,256]{1,0:T(8,128)S(1)}, f32[264,256]{1,0:T(8,128)S(1)}, u32[]{:S(2)}, u32[]{:S(2)}) collective-permute-start(f32[264,256]{1,0:T(8,128)S(1)} %get-tuple-element.19), channel_id=1, source_target_pairs={{1,2},{3,4},{5,6},{7,8},{9,10},{11,12},{13,14},{15,16},{17,18},{19... | collective-permute-start | bytes 811016 | tf_op jit(solution)/shard_map/ppermute | solution.py:303
  102.7 0.0 collective-permute-done.4.got_ref
  102.7 2.4 %local_bands.1 = (f32[768,768]{1,0:T(8,128)}, f32[768,512]{1,0:T(8,128)}) custom-call(f32[9,256,256]{2,1,0:T(8,128)S(1)} %get-tuple-element.20.keep_ref, f32[9,256,256]{2,1,0:T(8,128)S(1)} %collective-permute-done.4.got_ref), custom_call_target="tpu_custom_call" | custom-call | flops 10000000 | bytes 12000000 | tf_op jit(solution)/shard_map/local_bands/pallas_call | solution.py:189
  105.0 3.8 %collective-permute-done.3.cross_ref = f32[264,256]{1,0:T(8,128)S(1)} collective-permute-done((f32[264,256]{1,0:T(8,128)S(1)}, f32[264,256]{1,0:T(8,128)S(1)}, u32[]{:S(2)}, u32[]{:S(2)}) %collective-permute-start.3) | collective-permute-done | bytes 270368 | tf_op jit(solution)/shard_map/ppermute | solution.py:303
  108.9 0.7 copy-done.3
  109.6 2.1 %finish.1 = (f32[768,768]{1,0:T(8,128)}, f32[768,512]{1,0:T(8,128)}) custom-call(f32[512,256]{1,0:T(8,128)} %copy-done, f32[264,256]{1,0:T(8,128)} %copy-done.3, f32[8,256]{1,0:T(8,128)} %copy-done.1, f32[768,768]{1,0:T(8,128)} %get-tuple-element.22._, f32[768,512]{1,0:T(8,128)} %get-tuple-element.23.__), custom_call_target="tpu_custom_call", output_to_operand_aliasing={{0}: (3, {}), {1}: (4, {})} | custom-call | tf_op jit(solution)/shard_map/finish/pallas_call | solution.py:268
  (2 shorter events, 0.0 us)
Async XLA Ops:
  0.6 58.2 %copy-start.2 = (s32[6,2]{0,1:T(2,128)S(1)}, s32[6,2]{0,1:T(2,128)}, u32[]{:S(2)}) copy-start(s32[6,2]{0,1:T(2,128)} %param.3) | copy-start | bytes 148
  48.3 32.1 %collective-permute-start = (bf16[3000,256]{1,0:T(8,128)(2,1)S(1)}, bf16[3000,256]{1,0:T(8,128)(2,1)S(1)}, u32[]{:S(2)}, u32[]{:S(2)}) collective-permute-start(bf16[3000,256]{1,0:T(8,128)(2,1)S(1)} %get-tuple-element.13), channel_id=1, source_target_pairs={{2,0},{4,2},{6,4},{8,6},{10,8},{12,10},{14,12},{16,14},{18,16},{20... | collective-permute-start | bytes 4608008 | tf_op jit(solution)/shard_map/ppermute | solution.py:296
  58.8 10.1 %copy-start.4 = (bf16[3000,256]{1,0:T(8,128)(2,1)S(1)}, bf16[3000,256]{1,0:T(8,128)(2,1)}, u32[]{:S(2)}) copy-start(bf16[3000,256]{1,0:T(8,128)(2,1)} %get-tuple-element.15) | copy-start | bytes 4608004
  68.8 26.3 %copy-start.1 = (f32[8,256]{1,0:T(8,128)}, f32[8,256]{1,0:T(8,128)S(1)}, u32[]{:S(2)}) copy-start(f32[8,256]{1,0:T(8,128)S(1)} %get-tuple-element.17.mask_ref) | copy-start | bytes 24580
  68.8 33.9 %collective-permute-start.4 = (f32[9,256,256]{2,1,0:T(8,128)S(1)}, f32[9,256,256]{2,1,0:T(8,128)S(1)}, u32[]{:S(2)}, u32[]{:S(2)}) collective-permute-start(f32[9,256,256]{2,1,0:T(8,128)S(1)} %get-tuple-element.21), channel_id=1, source_target_pairs={{0,1},{1,0},{2,3},{3,2},{4,5},{5,4},{6,7},{7,6},{8,9},{9,8},{10,11... | collective-permute-start | bytes 7077896 | tf_op jit(solution)/shard_map/ppermute | solution.py:301
  68.9 26.1 %collective-permute-start.1 = (bf16[3000,256]{1,0:T(8,128)(2,1)S(1)}, bf16[3000,256]{1,0:T(8,128)(2,1)S(1)}, u32[]{:S(2)}, u32[]{:S(2)}) collective-permute-start(bf16[3000,256]{1,0:T(8,128)(2,1)S(1)} %copy-done.4), channel_id=1, source_target_pairs={{0,2},{2,4},{4,6},{6,8},{8,10},{10,12},{12,14},{14,16},{16,18},{18... | collective-permute-start | bytes 4608008 | tf_op jit(solution)/shard_map/ppermute | solution.py:297
  84.3 10.8 %collective-permute-start.2 = (f32[512,256]{1,0:T(8,128)S(1)}, f32[512,256]{1,0:T(8,128)S(1)}, u32[]{:S(2)}, u32[]{:S(2)}) collective-permute-start(f32[512,256]{1,0:T(8,128)S(1)} %get-tuple-element.16), channel_id=1, source_target_pairs={{0,1},{1,0},{2,3},{3,2},{4,5},{5,4},{6,7},{7,6},{8,9},{9,8},{10,11... | collective-permute-start | bytes 1572872 | tf_op jit(solution)/shard_map/ppermute | solution.py:299
  96.1 0.8 copy-start
  96.9 12.0 %collective-permute-start.3 = (f32[264,256]{1,0:T(8,128)S(1)}, f32[264,256]{1,0:T(8,128)S(1)}, u32[]{:S(2)}, u32[]{:S(2)}) collective-permute-start(f32[264,256]{1,0:T(8,128)S(1)} %get-tuple-element.19), channel_id=1, source_target_pairs={{1,2},{3,4},{5,6},{7,8},{9,10},{11,12},{13,14},{15,16},{17,18},{19... | collective-permute-start | bytes 811016 | tf_op jit(solution)/shard_map/ppermute | solution.py:303
  108.9 0.7 copy-start.3

commit v3 on v2

--- a/solution.py
+++ b/solution.py
@@ -21,36 +21,27 @@
 OVER_ROWS = (((0,), (0,)), ((), ()))
 
 
-def cut_kernel(g_ref, one_ref, two_ref, sems):
-    core = lax.axis_index("aux")
-    last = (BLOCKS - 1) * BS
-    moves = [
-        pltpu.make_async_copy(
-            g_ref.at[:, pl.ds(pl.multiple_of(start, BS), BS)], out, sems.at[i]
-        )
-        for i, (start, out) in enumerate(((core * last, one_ref), ((1 - core) * last, two_ref)))
-    ]
-    for move in moves:
-        move.start()
-    for move in moves:
-        move.wait()
+def cut_kernel(g_ref, out_ref, sem):
+    start = pl.multiple_of(lax.axis_index("aux") * ((BLOCKS - 1) * BS), BS)
+    move = pltpu.make_async_copy(g_ref.at[:, pl.ds(start, BS)], out_ref, sem)
+    move.start()
+    move.wait()
 
 
 def cut(g):
-    out = jax.ShapeDtypeStruct((g.shape[0], BS), g.dtype)
     return pl.pallas_call(
         cut_kernel,
         in_specs=[ANY],
-        out_specs=[ANY, ANY],
-        out_shape=[out, out],
-        scratch_shapes=[pltpu.SemaphoreType.DMA((2,))],
+        out_specs=VMEM,
+        out_shape=jax.ShapeDtypeStruct((g.shape[0], BS), g.dtype),
+        scratch_shapes=[pltpu.SemaphoreType.DMA(())],
         compiler_params=pltpu.CompilerParams(vmem_limit_bytes=52 * MIB),
         cost_estimate=pl.CostEstimate(flops=0, bytes_accessed=3_000_000, transcendentals=0),
         name="cut",
     )(g)
 
 
-def local_kernel(flags, g_ref, keep_ref, give_ref, mask_ref, held, sems):
+def local_kernel(flags, g_ref, keep_ref, give_ref, mask_ref, two_ref, held, sems):
     core = lax.axis_index("aux")
     loads = []
     for block in range(BLOCKS):
@@ -59,10 +50,15 @@
     for load in reversed(loads):
         load.start()
 
+    start = pl.multiple_of((1 - core) * ((BLOCKS - 1) * BS), BS)
+    second = pltpu.make_async_copy(g_ref.at[:, pl.ds(start, BS)], two_ref, sems.at[BLOCKS])
+    second.start()
+
     row = lax.broadcasted_iota(jnp.int32, (8, BS), 0)
     near, far, other = flags[0, BLOCKS - 1], flags[1, BLOCKS - 1], flags[1, BLOCKS - 2]
     values = jnp.where(row == 0, near, jnp.where(row == 1, far, other))
-    mask_ref[...] = values.astype(jnp.float32)
+    inside = lax.axis_index("ao") < lax.axis_size("ao") - 1
+    mask_ref[...] = jnp.where(inside, values, 0).astype(jnp.float32)
 
     def row_of_tiles(m, count):
         left = held[:, pl.ds(pl.multiple_of(m * BS, BS), BS)]
@@ -106,6 +102,7 @@
         return carry
 
     lax.fori_loop(0, BLOCKS - 2, step, 0)
+    second.wait()
 
 
 def local_tiles(flags, g):
@@ -113,15 +110,16 @@
     return pl.pallas_call(
         local_kernel,
         in_specs=[SMEM, ANY],
-        out_specs=[VMEM, VMEM, VMEM],
+        out_specs=[VMEM, VMEM, VMEM, VMEM],
         out_shape=[
             jax.ShapeDtypeStruct((SLOTS, BS, BS), jnp.float32),
             jax.ShapeDtypeStruct((SLOTS, BS, BS), jnp.float32),
             jax.ShapeDtypeStruct((8, BS), jnp.float32),
+            jax.ShapeDtypeStruct((nocc, BS), jnp.bfloat16),
         ],
         scratch_shapes=[
             pltpu.VMEM((nocc, BLOCKS * BS), jnp.bfloat16),
-            pltpu.SemaphoreType.DMA((BLOCKS,)),
+            pltpu.SemaphoreType.DMA((BLOCKS + 1,)),
         ],
         compiler_params=pltpu.CompilerParams(vmem_limit_bytes=44 * MIB),
         cost_estimate=pl.CostEstimate(
@@ -276,6 +274,7 @@
         input_output_aliases={3: 0, 4: 1},
         scratch_shapes=[pltpu.VMEM((BS, BS), jnp.float32)] * 3
         + [pltpu.SemaphoreType.DMA((3,))],
+        compiler_params=pltpu.CompilerParams(vmem_limit_bytes=8 * MIB),
         name="finish",
     )(total, crossed, mask, upper, lower)
 
@@ -283,21 +282,19 @@
 def body(factors, pair_keep):
     chips = lax.axis_size("ao")
     axes = ("ao", "aux")
-    edges = [(c, c + 1) for c in range(chips - 1)]
+    edges = [(c, (c + 1) % chips) for c in range(chips)]
     leg_one = [(2 * b, 2 * a) for a, b in edges] + [(2 * a + 1, 2 * b + 1) for a, b in edges]
     leg_two = [(2 * a, 2 * b) for a, b in edges] + [(2 * b + 1, 2 * a + 1) for a, b in edges]
     swap = [(2 * c + k, 2 * c + 1 - k) for c in range(chips) for k in range(2)]
-    ahead = [(2 * a + 1, 2 * b) for a, b in edges]
-    cross = ahead + [(b, a) for a, b in ahead]
+    cross = [(2 * a + 1, 2 * b) for a, b in edges] + [(2 * b, 2 * a + 1) for a, b in edges]
 
     g = jnp.swapaxes(factors[0], 0, 1)
     flags = jnp.swapaxes(pair_keep, 0, 1)
-    one, two = cut(g)
-    came_one = lax.ppermute(one, axes, leg_one)
+    came_one = lax.ppermute(cut(g), axes, leg_one)
+    keep, give, mask, two = local_tiles(flags, g)
     came_two = lax.ppermute(two, axes, leg_two)
     edge_give, turned = edge_partial(g, came_one)
     edge_got = lax.ppermute(edge_give, axes, swap)
-    keep, give, mask = local_tiles(flags, g)
     got = lax.ppermute(give, axes, swap)
     total, send = edge_sum(turned, came_two, edge_got, mask)
     crossed = lax.ppermute(send, axes, cross)

time: 112 us -> 60 us (0.54)
  the two profiles are of different devices: /device:TPU:6 before, /device:TPU:0 now
where the time goes in v3:
time: 60 us; the launch traced here: 59.9 us
  waiting for transfers between devices  24.7 us (41%)
  Pallas kernels  19.6 us (33%)
  starting transfers between devices  14.9 us (25%)
  between operations  0.69 us (1%)
    ppermute x1, waiting for transfers between devices, body(): came_one = lax.ppermute(cut(g), axes, leg_one)  13.4 us
    pallas_call x1, Pallas kernels, local_tiles(): pl.pallas_call(local_kernel, in_specs=[SMEM, ANY], out_specs=[VMEM, VMEM,...  9.98 us
    ppermute x1, starting transfers between devices, body(): came_one = lax.ppermute(cut(g), axes, leg_one)  8.84 us
    ppermute x1, waiting for transfers between devices, body(): came_two = lax.ppermute(two, axes, leg_two)  8.09 us
    ppermute x1, starting transfers between devices, body(): crossed = lax.ppermute(send, axes, cross)  5.8 us
    pallas_call x1, Pallas kernels, edge_partial(): pl.pallas_call(edge_kernel, in_specs=[ANY, VMEM], out_specs=[VMEM, VMEM],...  3.85 us
    ppermute x1, waiting for transfers between devices, body(): crossed = lax.ppermute(send, axes, cross)  3.24 us
    pallas_call x1, Pallas kernels, local_bands(): pl.pallas_call(band_kernel, in_specs=[VMEM, VMEM], out_specs=[VMEM, VMEM]...  2.36 us
  transfers between devices with their start and end apart: 5, of which 3 were waited for; matrix products, arithmetic and copies ran while one was open for 0% of the time, Pallas kernels for 29%

profile of v3, /device:TPU:0, one launch (start us, length us, event | category | flops | bytes accessed | tf_op | source)
XLA Modules:
  0.0 59.9 jit_solution(5532892936771803050)
XLA Ops:
  0.6 0.0 copy-start
  0.6 1.4 %cut.1 = bf16[3000,256]{1,0:T(8,128)(2,1)S(1)} custom-call(bf16[3000,1536]{1,0:T(8,128)(2,1)} %bitcast.5), custom_call_target="tpu_custom_call" | custom-call | bytes 3000000 | tf_op jit(solution)/shard_map/cut/pallas_call | solution.py:32
  2.1 8.8 %collective-permute-start = (bf16[3000,256]{1,0:T(8,128)(2,1)S(1)}, bf16[3000,256]{1,0:T(8,128)(2,1)S(1)}, u32[]{:S(2)}, u32[]{:S(2)}) collective-permute-start(bf16[3000,256]{1,0:T(8,128)(2,1)S(1)} %cut.1), channel_id=1, source_target_pairs={{2,0},{4,2},{6,4},{8,6},{10,8},{12,10},{14,12},{16,14},{18,16},{20... | collective-permute-start | bytes 4608008 | tf_op jit(solution)/shard_map/ppermute | solution.py:293
  10.9 0.0 copy-done
  10.9 10.0 %local_tiles.1 = (f32[9,256,256]{2,1,0:T(8,128)S(1)}, f32[9,256,256]{2,1,0:T(8,128)S(1)}, f32[8,256]{1,0:T(8,128)S(1)}, bf16[3000,256]{1,0:T(8,128)(2,1)S(1)}) custom-call(s32[2,6]{1,0:T(2,128)S(1)} %bitcast.4, bf16[3000,1536]{1,0:T(8,128)(2,1)} %bitcast.6), custom_call_target="tpu_custom_call" | custom-call | flops 12000000000 | bytes 20000000 | tf_op jit(solution)/shard_map/local_tiles/pallas_call | solution.py:110
  20.9 0.1 collective-permute-start.4
  21.0 0.1 collective-permute-start.1
  21.1 13.4 %collective-permute-done.came_ref = bf16[3000,256]{1,0:T(8,128)(2,1)S(1)} collective-permute-done((bf16[3000,256]{1,0:T(8,128)(2,1)S(1)}, bf16[3000,256]{1,0:T(8,128)(2,1)S(1)}, u32[]{:S(2)}, u32[]{:S(2)}) %collective-permute-start) | collective-permute-done | bytes 1536032 | tf_op jit(solution)/shard_map/ppermute | solution.py:293
  34.5 3.9 %edge_partial.1 = (f32[512,256]{1,0:T(8,128)S(1)}, bf16[512,3000]{1,0:T(8,128)(2,1)S(1)}) custom-call(bf16[3000,1536]{1,0:T(8,128)(2,1)} %bitcast.7, bf16[3000,256]{1,0:T(8,128)(2,1)S(1)} %collective-permute-done.came_ref), custom_call_target="tpu_custom_call" | custom-call | flops 1600000000 | bytes 8000000 | tf_op jit(solution)/shard_map/edge_partial/pallas_call | solution.py:151
  38.3 0.1 collective-permute-start.2
  38.4 8.1 %collective-permute-done.1.came_ref = bf16[3000,256]{1,0:T(8,128)(2,1)S(1)} collective-permute-done((bf16[3000,256]{1,0:T(8,128)(2,1)S(1)}, bf16[3000,256]{1,0:T(8,128)(2,1)S(1)}, u32[]{:S(2)}, u32[]{:S(2)}) %collective-permute-start.1) | collective-permute-done | bytes 1536032 | tf_op jit(solution)/shard_map/ppermute | solution.py:295
  46.5 0.0 collective-permute-done.2.got_ref
  46.5 1.0 %edge_sum.1 = (f32[512,256]{1,0:T(8,128)S(1)}, f32[264,256]{1,0:T(8,128)S(1)}) custom-call(bf16[512,3000]{1,0:T(8,128)(2,1)S(1)} %get-tuple-element.12.turned_ref, bf16[3000,256]{1,0:T(8,128)(2,1)S(1)} %collective-permute-done.1.came_ref, f32[512,256]{1,0:T(8,128)S(1)} %collective-permute-done.2.got_ref, f32[8,256]{1,0:T(8,128)S(1)} %get-tuple-element.15.mask_ref), custom_call_target="tpu_custom_call" | custom-call | flops 1600000000 | bytes 5000000 | tf_op jit(solution)/shard_map/edge_sum/pallas_call | solution.py:217
  47.6 5.8 %collective-permute-start.3 = (f32[264,256]{1,0:T(8,128)S(1)}, f32[264,256]{1,0:T(8,128)S(1)}, u32[]{:S(2)}, u32[]{:S(2)}) collective-permute-start(f32[264,256]{1,0:T(8,128)S(1)} %get-tuple-element.17), channel_id=1, source_target_pairs={{1,2},{3,4},{5,6},{7,8},{9,10},{11,12},{13,14},{15,16},{17,18},{19... | collective-permute-start | bytes 811016 | tf_op jit(solution)/shard_map/ppermute | solution.py:300
  53.4 0.0 collective-permute-done.4.got_ref
  53.4 2.4 %local_bands.1 = (f32[768,768]{1,0:T(8,128)}, f32[768,512]{1,0:T(8,128)}) custom-call(f32[9,256,256]{2,1,0:T(8,128)S(1)} %get-tuple-element.18.keep_ref, f32[9,256,256]{2,1,0:T(8,128)S(1)} %collective-permute-done.4.got_ref), custom_call_target="tpu_custom_call" | custom-call | flops 10000000 | bytes 12000000 | tf_op jit(solution)/shard_map/local_bands/pallas_call | solution.py:187
  55.7 3.2 %collective-permute-done.3.cross_ref = f32[264,256]{1,0:T(8,128)S(1)} collective-permute-done((f32[264,256]{1,0:T(8,128)S(1)}, f32[264,256]{1,0:T(8,128)S(1)}, u32[]{:S(2)}, u32[]{:S(2)}) %collective-permute-start.3) | collective-permute-done | bytes 270368 | tf_op jit(solution)/shard_map/ppermute | solution.py:300
  59.0 0.9 %finish.1 = (f32[768,768]{1,0:T(8,128)}, f32[768,512]{1,0:T(8,128)}) custom-call(f32[512,256]{1,0:T(8,128)S(1)} %get-tuple-element.16.sum_ref, f32[264,256]{1,0:T(8,128)S(1)} %collective-permute-done.3.cross_ref, f32[8,256]{1,0:T(8,128)S(1)} %get-tuple-element.15.mask_ref, ...), custom_call_target="tpu_custom_call", output_to_operand_aliasing={{0}: (3, {}), {1}: (4, {})} | custom-call | tf_op jit(solution)/shard_map/finish/pallas_call | solution.py:266
Async XLA Ops:
  0.6 10.3 %copy-start = (s32[6,2]{0,1:T(2,128)S(1)}, s32[6,2]{0,1:T(2,128)}, u32[]{:S(2)}) copy-start(s32[6,2]{0,1:T(2,128)} %param.3) | copy-start | bytes 148
  2.1 32.4 %collective-permute-start = (bf16[3000,256]{1,0:T(8,128)(2,1)S(1)}, bf16[3000,256]{1,0:T(8,128)(2,1)S(1)}, u32[]{:S(2)}, u32[]{:S(2)}) collective-permute-start(bf16[3000,256]{1,0:T(8,128)(2,1)S(1)} %cut.1), channel_id=1, source_target_pairs={{2,0},{4,2},{6,4},{8,6},{10,8},{12,10},{14,12},{16,14},{18,16},{20... | collective-permute-start | bytes 4608008 | tf_op jit(solution)/shard_map/ppermute | solution.py:293
  20.9 32.5 %collective-permute-start.4 = (f32[9,256,256]{2,1,0:T(8,128)S(1)}, f32[9,256,256]{2,1,0:T(8,128)S(1)}, u32[]{:S(2)}, u32[]{:S(2)}) collective-permute-start(f32[9,256,256]{2,1,0:T(8,128)S(1)} %get-tuple-element.19), channel_id=1, source_target_pairs={{0,1},{1,0},{2,3},{3,2},{4,5},{5,4},{6,7},{7,6},{8,9},{9,8},{10,11... | collective-permute-start | bytes 7077896 | tf_op jit(solution)/shard_map/ppermute | solution.py:298
  21.0 25.5 %collective-permute-start.1 = (bf16[3000,256]{1,0:T(8,128)(2,1)S(1)}, bf16[3000,256]{1,0:T(8,128)(2,1)S(1)}, u32[]{:S(2)}, u32[]{:S(2)}) collective-permute-start(bf16[3000,256]{1,0:T(8,128)(2,1)S(1)} %get-tuple-element.13), channel_id=1, source_target_pairs={{0,2},{2,4},{4,6},{6,8},{8,10},{10,12},{12,14},{14,16},{16,18},{18... | collective-permute-start | bytes 4608008 | tf_op jit(solution)/shard_map/ppermute | solution.py:295
  38.3 8.2 %collective-permute-start.2 = (f32[512,256]{1,0:T(8,128)S(1)}, f32[512,256]{1,0:T(8,128)S(1)}, u32[]{:S(2)}, u32[]{:S(2)}) collective-permute-start(f32[512,256]{1,0:T(8,128)S(1)} %get-tuple-element.14), channel_id=1, source_target_pairs={{0,1},{1,0},{2,3},{3,2},{4,5},{5,4},{6,7},{7,6},{8,9},{9,8},{10,11... | collective-permute-start | bytes 1572872 | tf_op jit(solution)/shard_map/ppermute | solution.py:297
  47.6 11.4 %collective-permute-start.3 = (f32[264,256]{1,0:T(8,128)S(1)}, f32[264,256]{1,0:T(8,128)S(1)}, u32[]{:S(2)}, u32[]{:S(2)}) collective-permute-start(f32[264,256]{1,0:T(8,128)S(1)} %get-tuple-element.17), channel_id=1, source_target_pairs={{1,2},{3,4},{5,6},{7,8},{9,10},{11,12},{13,14},{15,16},{17,18},{19... | collective-permute-start | bytes 811016 | tf_op jit(solution)/shard_map/ppermute | solution.py:300

commit v4 on v3

--- a/solution.py
+++ b/solution.py
@@ -1,3 +1,5 @@
+import functools
+
 import jax
 import jax.numpy as jnp
 from jax import lax
@@ -21,27 +23,30 @@
 OVER_ROWS = (((0,), (0,)), ((), ()))
 
 
-def cut_kernel(g_ref, out_ref, sem):
-    start = pl.multiple_of(lax.axis_index("aux") * ((BLOCKS - 1) * BS), BS)
-    move = pltpu.make_async_copy(g_ref.at[:, pl.ds(start, BS)], out_ref, sem)
+def cut_kernel(g_ref, out_ref, sem, *, swapped):
+    core = lax.axis_index("aux")
+    count = out_ref.shape[1]
+    start = (1 - core if swapped else core) * (BLOCKS * BS - count)
+    cols = pl.ds(pl.multiple_of(start, BS), count)
+    move = pltpu.make_async_copy(g_ref.at[:, cols], out_ref, sem)
     move.start()
     move.wait()
 
 
-def cut(g):
-    return pl.pallas_call(
-        cut_kernel,
+def cut(name, g, blocks, swapped):
+    return pl.pallas_call(
+        functools.partial(cut_kernel, swapped=swapped),
         in_specs=[ANY],
         out_specs=VMEM,
-        out_shape=jax.ShapeDtypeStruct((g.shape[0], BS), g.dtype),
+        out_shape=jax.ShapeDtypeStruct((g.shape[0], blocks * BS), g.dtype),
         scratch_shapes=[pltpu.SemaphoreType.DMA(())],
         compiler_params=pltpu.CompilerParams(vmem_limit_bytes=52 * MIB),
-        cost_estimate=pl.CostEstimate(flops=0, bytes_accessed=3_000_000, transcendentals=0),
-        name="cut",
+        cost_estimate=pl.CostEstimate(flops=0, bytes_accessed=1000, transcendentals=0),
+        name=name,
     )(g)
 
 
-def local_kernel(flags, g_ref, keep_ref, give_ref, mask_ref, two_ref, held, sems):
+def local_kernel(flags, g_ref, keep_ref, give_ref, mask_ref, wide_ref, held, sems):
     core = lax.axis_index("aux")
     loads = []
     for block in range(BLOCKS):
@@ -50,9 +55,9 @@
     for load in reversed(loads):
         load.start()
 
-    start = pl.multiple_of((1 - core) * ((BLOCKS - 1) * BS), BS)
-    second = pltpu.make_async_copy(g_ref.at[:, pl.ds(start, BS)], two_ref, sems.at[BLOCKS])
-    second.start()
+    start = pl.multiple_of(core * ((BLOCKS - 2) * BS), BS)
+    wide = pltpu.make_async_copy(g_ref.at[:, pl.ds(start, 2 * BS)], wide_ref, sems.at[BLOCKS])
+    wide.start()
 
     row = lax.broadcasted_iota(jnp.int32, (8, BS), 0)
     near, far, other = flags[0, BLOCKS - 1], flags[1, BLOCKS - 1], flags[1, BLOCKS - 2]
@@ -102,7 +107,7 @@
         return carry
 
     lax.fori_loop(0, BLOCKS - 2, step, 0)
-    second.wait()
+    wide.wait()
 
 
 def local_tiles(flags, g):
@@ -115,7 +120,7 @@
             jax.ShapeDtypeStruct((SLOTS, BS, BS), jnp.float32),
             jax.ShapeDtypeStruct((SLOTS, BS, BS), jnp.float32),
             jax.ShapeDtypeStruct((8, BS), jnp.float32),
-            jax.ShapeDtypeStruct((nocc, BS), jnp.bfloat16),
+            jax.ShapeDtypeStruct((nocc, 2 * BS), jnp.bfloat16),
         ],
         scratch_shapes=[
             pltpu.VMEM((nocc, BLOCKS * BS), jnp.bfloat16),
@@ -123,47 +128,28 @@
         ],
         compiler_params=pltpu.CompilerParams(vmem_limit_bytes=44 * MIB),
         cost_estimate=pl.CostEstimate(
-            flops=12_000_000_000, bytes_accessed=20_000_000, transcendentals=0
+            flops=100_000_000_000, bytes_accessed=1000, transcendentals=0
         ),
         name="local_tiles",
     )(flags, g)
 
 
-def edge_kernel(g_ref, came_ref, give_ref, turned_ref, one, two, sems):
-    core = lax.axis_index("aux")
-    far = (BLOCKS - 2) * BS
-    loads = []
-    for i, (start, held) in enumerate((((1 - core) * far, one), (core * far, two))):
-        cols = pl.ds(pl.multiple_of(start, BS), 2 * BS)
-        loads.append(pltpu.make_async_copy(g_ref.at[:, cols], held, sems.at[i]))
-    for load in loads:
-        load.start()
-    loads[0].wait()
-    give_ref[...] = lax.dot_general(
-        one[...], came_ref[...], OVER_ROWS, preferred_element_type=jnp.float32
+def edge_kernel(came_ref, wide_ref, part_ref):
+    part_ref[...] = lax.dot_general(
+        came_ref[...], wide_ref[...], OVER_ROWS, preferred_element_type=jnp.float32
     )
-    loads[1].wait()
-    turned_ref[...] = two[...].T
-
-
-def edge_partial(g, came):
-    nocc = g.shape[0]
+
+
+def edge_partial(came, wide):
     return pl.pallas_call(
         edge_kernel,
-        in_specs=[ANY, VMEM],
-        out_specs=[VMEM, VMEM],
-        out_shape=[
-            jax.ShapeDtypeStruct((2 * BS, BS), jnp.float32),
-            jax.ShapeDtypeStruct((2 * BS, nocc), jnp.bfloat16),
-        ],
-        scratch_shapes=[pltpu.VMEM((nocc, 2 * BS), jnp.bfloat16)] * 2
-        + [pltpu.SemaphoreType.DMA((2,))],
-        compiler_params=pltpu.CompilerParams(vmem_limit_bytes=44 * MIB),
-        cost_estimate=pl.CostEstimate(
-            flops=1_600_000_000, bytes_accessed=8_000_000, transcendentals=0
-        ),
+        in_specs=[VMEM, VMEM],
+        out_specs=VMEM,
+        out_shape=jax.ShapeDtypeStruct((BS, 2 * BS), jnp.float32),
+        compiler_params=pltpu.CompilerParams(vmem_limit_bytes=16 * MIB),
+        cost_estimate=pl.CostEstimate(flops=0, bytes_accessed=1000, transcendentals=0),
         name="edge_partial",
-    )(g, came)
+    )(came, wide)
 
 
 def band_kernel(keep_ref, got_ref, upper_ref, lower_ref):
@@ -200,20 +186,22 @@
     )(keep, got)
 
 
-def sum_kernel(turned_ref, came_ref, got_ref, mask_ref, sum_ref, send_ref):
-    total = jnp.dot(turned_ref[...], came_ref[...], preferred_element_type=jnp.float32)
+def sum_kernel(came_ref, wide_ref, part_ref, mask_ref, sum_ref, send_ref):
+    total = part_ref[...] + lax.dot_general(
+        came_ref[...], wide_ref[...], OVER_ROWS, preferred_element_type=jnp.float32
+    )
     first = lax.axis_index("aux") == 0
     near = jnp.where(first, 1.0, mask_ref[0:1, :])
     other_pair = jnp.where(first, 1.0, mask_ref[2:3, :])
-    top = jnp.where(other_pair > 0, total[:BS] + got_ref[:BS], 0.0)
-    low = jnp.where(near > 0, total[BS:] + got_ref[BS:], 0.0)
-    sum_ref[:BS] = top
-    sum_ref[BS:] = low
-    send_ref[:BS] = jnp.where(first, low, top).T
-    send_ref[BS:] = mask_ref[...]
-
-
-def edge_sum(turned, came, got, mask):
+    left = jnp.where(other_pair > 0, total[:, :BS], 0.0)
+    right = jnp.where(near > 0, total[:, BS:], 0.0)
+    send_ref[:BS] = jnp.where(first, right, left)
+    send_ref[BS:] = jnp.where(first, 0.0, mask_ref[...])
+    sum_ref[:BS] = left.T
+    sum_ref[BS:] = right.T
+
+
+def edge_sum(came, wide, part, mask):
     return pl.pallas_call(
         sum_kernel,
         in_specs=[VMEM] * 4,
@@ -224,10 +212,10 @@
         ],
         compiler_params=pltpu.CompilerParams(vmem_limit_bytes=16 * MIB),
         cost_estimate=pl.CostEstimate(
-            flops=1_600_000_000, bytes_accessed=5_000_000, transcendentals=0
+            flops=50_000_000_000, bytes_accessed=1000, transcendentals=0
         ),
         name="edge_sum",
-    )(turned, came, got, mask)
+    )(came, wide, part, mask)
 
 
 def finish_kernel(sum_ref, cross_ref, mask_ref, _, __, upper_ref, lower_ref, *scratch):
@@ -236,7 +224,7 @@
     first = core == 0
     near = jnp.where(first, cross_ref[BS:BS + 1, :], 1.0)
     far = jnp.where(first, cross_ref[BS + 1:BS + 2, :], 1.0)
-    third = jnp.where(first, 1.0, mask_ref[1:2, :])
+    third = jnp.where(first, cross_ref[BS + 2:BS + 3, :], mask_ref[1:2, :])
     stages[0][...] = jnp.where(near > 0, sum_ref[:BS], 0.0)
     stages[1][...] = jnp.where(far > 0, sum_ref[BS:], 0.0)
     stages[2][...] = jnp.where(third > 0, cross_ref[:BS], 0.0)
@@ -282,21 +270,23 @@
 def body(factors, pair_keep):
     chips = lax.axis_size("ao")
     axes = ("ao", "aux")
-    edges = [(c, (c + 1) % chips) for c in range(chips)]
-    leg_one = [(2 * b, 2 * a) for a, b in edges] + [(2 * a + 1, 2 * b + 1) for a, b in edges]
-    leg_two = [(2 * a, 2 * b) for a, b in edges] + [(2 * b + 1, 2 * a + 1) for a, b in edges]
+    edges = [(c, c + 1) for c in range(chips - 1)]
+    low, high = 0, 2 * chips - 1
+    cross = [(2 * a + 1, 2 * b) for a, b in edges] + [(high, low)]
+    cross = cross + [(b, a) for a, b in cross]
+    along = [(2 * a, 2 * b) for a, b in edges] + [(2 * b + 1, 2 * a + 1) for a, b in edges]
+    along = along + [(low + 1, low), (high - 1, high)]
     swap = [(2 * c + k, 2 * c + 1 - k) for c in range(chips) for k in range(2)]
-    cross = [(2 * a + 1, 2 * b) for a, b in edges] + [(2 * b, 2 * a + 1) for a, b in edges]
 
     g = jnp.swapaxes(factors[0], 0, 1)
     flags = jnp.swapaxes(pair_keep, 0, 1)
-    came_one = lax.ppermute(cut(g), axes, leg_one)
-    keep, give, mask, two = local_tiles(flags, g)
-    came_two = lax.ppermute(two, axes, leg_two)
-    edge_give, turned = edge_partial(g, came_one)
-    edge_got = lax.ppermute(edge_give, axes, swap)
+    came_one = lax.ppermute(cut("cut_first", g, 1, True), axes, along)
+    came_two = lax.ppermute(cut("cut_second", g, 1, False), axes, cross)
+    other = lax.ppermute(cut("cut_wide", g, 2, True), axes, swap)
+    keep, give, mask, wide = local_tiles(flags, g)
     got = lax.ppermute(give, axes, swap)
-    total, send = edge_sum(turned, came_two, edge_got, mask)
+    part = edge_partial(came_one, wide)
+    total, send = edge_sum(came_two, other, part, mask)
     crossed = lax.ppermute(send, axes, cross)
     upper, lower = local_bands(keep, got)
     return tuple(finish(total, crossed, mask, upper, lower))

time: 60 us -> 57.6 us (0.960)
  the two profiles are of different devices: /device:TPU:0 before, /device:TPU:6 now
where the time goes in v4:
time: 57.6 us; the launch traced here: 57.4 us
  Pallas kernels  21.7 us (38%)
  waiting for transfers between devices  21.3 us (37%)
  starting transfers between devices  13.7 us (24%)
  between operations  0.7 us (1%)
    pallas_call x1, Pallas kernels, local_tiles(): pl.pallas_call(local_kernel, in_specs=[SMEM, ANY], out_specs=[VMEM, VMEM,...  9.99 us
    ppermute x1, waiting for transfers between devices, body(): came_two = lax.ppermute(cut('cut_second', g, 1, False), axes, cross)  9.39 us
    ppermute x1, waiting for transfers between devices, body(): came_one = lax.ppermute(cut('cut_first', g, 1, True), axes, along)  8.73 us
    ppermute x1, starting transfers between devices, body(): other = lax.ppermute(cut('cut_wide', g, 2, True), axes, swap)  6.63 us
    pallas_call x3, Pallas kernels, cut(): pl.pallas_call(functools.partial(cut_kernel, swapped=swapped), in_specs=[...  6.31 us
    ppermute x1, starting transfers between devices, body(): crossed = lax.ppermute(send, axes, cross)  4.62 us
    ppermute x1, waiting for transfers between devices, body(): crossed = lax.ppermute(send, axes, cross)  3.21 us
    pallas_call x1, Pallas kernels, local_bands(): pl.pallas_call(band_kernel, in_specs=[VMEM, VMEM], out_specs=[VMEM, VMEM]...  2.36 us
  transfers between devices with their start and end apart: 5, of which 3 were waited for; matrix products, arithmetic and copies ran while one was open for 0% of the time, Pallas kernels for 34%

profile of v4, /device:TPU:6, one launch (start us, length us, event | category | flops | bytes accessed | tf_op | source)
XLA Modules:
  0.0 57.4 jit_solution(13074578067537696859)
XLA Ops:
  0.6 1.4 %cut_first.1 = bf16[3000,256]{1,0:T(8,128)(2,1)S(1)} custom-call(bf16[3000,1536]{1,0:T(8,128)(2,1)} %bitcast.5), custom_call_target="tpu_custom_call" | custom-call | bytes 1000 | tf_op jit(solution)/shard_map/cut_first/pallas_call | solution.py:37
  2.0 1.7 %collective-permute-start.2 = (bf16[3000,256]{1,0:T(8,128)(2,1)S(1)}, bf16[3000,256]{1,0:T(8,128)(2,1)S(1)}, u32[]{:S(2)}, u32[]{:S(2)}) collective-permute-start(bf16[3000,256]{1,0:T(8,128)(2,1)S(1)} %cut_first.1), channel_id=1, source_target_pairs={{0,2},{2,4},{4,6},{6,8},{8,10},{10,12},{12,14},{14,16},{16,18},{18... | collective-permute-start | bytes 4608008 | tf_op jit(solution)/shard_map/ppermute | solution.py:283
  3.7 3.5 %cut_wide.1 = bf16[3000,512]{1,0:T(8,128)(2,1)} custom-call(bf16[3000,1536]{1,0:T(8,128)(2,1)} %bitcast.6), custom_call_target="tpu_custom_call" | custom-call | bytes 1000 | tf_op jit(solution)/shard_map/cut_wide/pallas_call | solution.py:37
  7.2 0.0 copy-start
  7.2 6.6 %collective-permute-start.1 = (bf16[3000,512]{1,0:T(8,128)(2,1)}, bf16[3000,512]{1,0:T(8,128)(2,1)S(1)}, u32[]{:S(2)}, u32[]{:S(2)}) collective-permute-start(bf16[3000,512]{1,0:T(8,128)(2,1)} %cut_wide.1), channel_id=1, source_target_pairs={{0,1},{1,0},{2,3},{3,2},{4,5},{5,4},{6,7},{7,6},{8,9},{9,8},{10,11... | collective-permute-start | bytes 9216008 | tf_op jit(solution)/shard_map/ppermute | solution.py:285
  13.9 1.4 %cut_second.1 = bf16[3000,256]{1,0:T(8,128)(2,1)S(1)} custom-call(bf16[3000,1536]{1,0:T(8,128)(2,1)} %bitcast.7), custom_call_target="tpu_custom_call" | custom-call | bytes 1000 | tf_op jit(solution)/shard_map/cut_second/pallas_call | solution.py:37
  15.3 0.7 %collective-permute-start = (bf16[3000,256]{1,0:T(8,128)(2,1)S(1)}, bf16[3000,256]{1,0:T(8,128)(2,1)S(1)}, u32[]{:S(2)}, u32[]{:S(2)}) collective-permute-start(bf16[3000,256]{1,0:T(8,128)(2,1)S(1)} %cut_second.1), channel_id=1, source_target_pairs={{1,2},{3,4},{5,6},{7,8},{9,10},{11,12},{13,14},{15,16},{17,18},{19... | collective-permute-start | bytes 4608008 | tf_op jit(solution)/shard_map/ppermute | solution.py:284
  15.9 0.0 copy-done
  15.9 10.0 %local_tiles.1 = (f32[9,256,256]{2,1,0:T(8,128)S(1)}, f32[9,256,256]{2,1,0:T(8,128)S(1)}, f32[8,256]{1,0:T(8,128)S(1)}, bf16[3000,512]{1,0:T(8,128)(2,1)S(1)}) custom-call(s32[2,6]{1,0:T(2,128)S(1)} %bitcast.4, bf16[3000,1536]{1,0:T(8,128)(2,1)} %bitcast.8), custom_call_target="tpu_custom_call" | custom-call | flops 99999997952 | bytes 1000 | tf_op jit(solution)/shard_map/local_tiles/pallas_call | solution.py:115
  25.9 0.1 collective-permute-start.4
  26.0 8.7 %collective-permute-done.2.came_ref = bf16[3000,256]{1,0:T(8,128)(2,1)S(1)} collective-permute-done((bf16[3000,256]{1,0:T(8,128)(2,1)S(1)}, bf16[3000,256]{1,0:T(8,128)(2,1)S(1)}, u32[]{:S(2)}, u32[]{:S(2)}) %collective-permute-start.2) | collective-permute-done | bytes 1536032 | tf_op jit(solution)/shard_map/ppermute | solution.py:283
  34.8 1.0 %edge_partial.1.part_ref = f32[256,512]{1,0:T(8,128)S(1)} custom-call(bf16[3000,256]{1,0:T(8,128)(2,1)S(1)} %collective-permute-done.2.came_ref, bf16[3000,512]{1,0:T(8,128)(2,1)S(1)} %get-tuple-element.10.wide_ref), custom_call_target="tpu_custom_call" | custom-call | bytes 1000 | tf_op jit(solution)/shard_map/edge_partial/pallas_call | solution.py:144
  35.8 9.4 %collective-permute-done.came_ref = bf16[3000,256]{1,0:T(8,128)(2,1)S(1)} collective-permute-done((bf16[3000,256]{1,0:T(8,128)(2,1)S(1)}, bf16[3000,256]{1,0:T(8,128)(2,1)S(1)}, u32[]{:S(2)}, u32[]{:S(2)}) %collective-permute-start) | collective-permute-done | bytes 1536032 | tf_op jit(solution)/shard_map/ppermute | solution.py:284
  45.2 0.0 collective-permute-done.1.wide_ref
  45.2 1.1 %edge_sum.1 = (f32[512,256]{1,0:T(8,128)S(1)}, f32[264,256]{1,0:T(8,128)S(1)}) custom-call(bf16[3000,256]{1,0:T(8,128)(2,1)S(1)} %collective-permute-done.came_ref, bf16[3000,512]{1,0:T(8,128)(2,1)S(1)} %collective-permute-done.1.wide_ref, f32[256,512]{1,0:T(8,128)S(1)} %edge_partial.1.part_ref, f32[8,256]{1,0:T(8,128)S(1)} %get-tuple-element.11.mask_ref), custom_call_target="tpu_custom_call" | custom-call | flops 49999998976 | bytes 1000 | tf_op jit(solution)/shard_map/edge_sum/pallas_call | solution.py:205
  46.3 4.6 %collective-permute-start.3 = (f32[264,256]{1,0:T(8,128)S(1)}, f32[264,256]{1,0:T(8,128)S(1)}, u32[]{:S(2)}, u32[]{:S(2)}) collective-permute-start(f32[264,256]{1,0:T(8,128)S(1)} %get-tuple-element.13), channel_id=1, source_target_pairs={{1,2},{3,4},{5,6},{7,8},{9,10},{11,12},{13,14},{15,16},{17,18},{19... | collective-permute-start | bytes 811016 | tf_op jit(solution)/shard_map/ppermute | solution.py:290
  50.9 0.0 collective-permute-done.4.got_ref
  50.9 2.4 %local_bands.1 = (f32[768,768]{1,0:T(8,128)}, f32[768,512]{1,0:T(8,128)}) custom-call(f32[9,256,256]{2,1,0:T(8,128)S(1)} %get-tuple-element.14.keep_ref, f32[9,256,256]{2,1,0:T(8,128)S(1)} %collective-permute-done.4.got_ref), custom_call_target="tpu_custom_call" | custom-call | flops 10000000 | bytes 12000000 | tf_op jit(solution)/shard_map/local_bands/pallas_call | solution.py:173
  53.3 3.2 %collective-permute-done.3.cross_ref = f32[264,256]{1,0:T(8,128)S(1)} collective-permute-done((f32[264,256]{1,0:T(8,128)S(1)}, f32[264,256]{1,0:T(8,128)S(1)}, u32[]{:S(2)}, u32[]{:S(2)}) %collective-permute-start.3) | collective-permute-done | bytes 270368 | tf_op jit(solution)/shard_map/ppermute | solution.py:290
  56.5 0.9 %finish.1 = (f32[768,768]{1,0:T(8,128)}, f32[768,512]{1,0:T(8,128)}) custom-call(f32[512,256]{1,0:T(8,128)S(1)} %get-tuple-element.12.sum_ref, f32[264,256]{1,0:T(8,128)S(1)} %collective-permute-done.3.cross_ref, f32[8,256]{1,0:T(8,128)S(1)} %get-tuple-element.11.mask_ref, ...), custom_call_target="tpu_custom_call", output_to_operand_aliasing={{0}: (3, {}), {1}: (4, {})} | custom-call | tf_op jit(solution)/shard_map/finish/pallas_call | solution.py:254
Async XLA Ops:
  2.0 32.7 %collective-permute-start.2 = (bf16[3000,256]{1,0:T(8,128)(2,1)S(1)}, bf16[3000,256]{1,0:T(8,128)(2,1)S(1)}, u32[]{:S(2)}, u32[]{:S(2)}) collective-permute-start(bf16[3000,256]{1,0:T(8,128)(2,1)S(1)} %cut_first.1), channel_id=1, source_target_pairs={{0,2},{2,4},{4,6},{6,8},{8,10},{10,12},{12,14},{14,16},{16,18},{18... | collective-permute-start | bytes 4608008 | tf_op jit(solution)/shard_map/ppermute | solution.py:283
  7.2 8.7 %copy-start = (s32[6,2]{0,1:T(2,128)S(1)}, s32[6,2]{0,1:T(2,128)}, u32[]{:S(2)}) copy-start(s32[6,2]{0,1:T(2,128)} %param.3) | copy-start | bytes 148
  7.2 37.9 %collective-permute-start.1 = (bf16[3000,512]{1,0:T(8,128)(2,1)}, bf16[3000,512]{1,0:T(8,128)(2,1)S(1)}, u32[]{:S(2)}, u32[]{:S(2)}) collective-permute-start(bf16[3000,512]{1,0:T(8,128)(2,1)} %cut_wide.1), channel_id=1, source_target_pairs={{0,1},{1,0},{2,3},{3,2},{4,5},{5,4},{6,7},{7,6},{8,9},{9,8},{10,11... | collective-permute-start | bytes 9216008 | tf_op jit(solution)/shard_map/ppermute | solution.py:285
  15.3 29.9 %collective-permute-start = (bf16[3000,256]{1,0:T(8,128)(2,1)S(1)}, bf16[3000,256]{1,0:T(8,128)(2,1)S(1)}, u32[]{:S(2)}, u32[]{:S(2)}) collective-permute-start(bf16[3000,256]{1,0:T(8,128)(2,1)S(1)} %cut_second.1), channel_id=1, source_target_pairs={{1,2},{3,4},{5,6},{7,8},{9,10},{11,12},{13,14},{15,16},{17,18},{19... | collective-permute-start | bytes 4608008 | tf_op jit(solution)/shard_map/ppermute | solution.py:284
  25.9 25.0 %collective-permute-start.4 = (f32[9,256,256]{2,1,0:T(8,128)S(1)}, f32[9,256,256]{2,1,0:T(8,128)S(1)}, u32[]{:S(2)}, u32[]{:S(2)}) collective-permute-start(f32[9,256,256]{2,1,0:T(8,128)S(1)} %get-tuple-element.15), channel_id=1, source_target_pairs={{0,1},{1,0},{2,3},{3,2},{4,5},{5,4},{6,7},{7,6},{8,9},{9,8},{10,11... | collective-permute-start | bytes 7077896 | tf_op jit(solution)/shard_map/ppermute | solution.py:287
  46.3 10.2 %collective-permute-start.3 = (f32[264,256]{1,0:T(8,128)S(1)}, f32[264,256]{1,0:T(8,128)S(1)}, u32[]{:S(2)}, u32[]{:S(2)}) collective-permute-start(f32[264,256]{1,0:T(8,128)S(1)} %get-tuple-element.13), channel_id=1, source_target_pairs={{1,2},{3,4},{5,6},{7,8},{9,10},{11,12},{13,14},{15,16},{17,18},{19... | collective-permute-start | bytes 811016 | tf_op jit(solution)/shard_map/ppermute | solution.py:290

commit v5 on v4

--- a/solution.py
+++ b/solution.py
@@ -10,6 +10,7 @@
 BS = 256
 BLOCKS = 6
 HELD = 3
+HALF = 128
 SLOTS = HELD * HELD
 MIB = 1024 * 1024
 
@@ -23,23 +24,29 @@
 OVER_ROWS = (((0,), (0,)), ((), ()))
 
 
-def cut_kernel(g_ref, out_ref, sem, *, swapped):
+def cut_kernel(g_ref, *refs, swapped):
+    outs, sems = refs[:-1], refs[-1]
+    count = outs[0].shape[1]
     core = lax.axis_index("aux")
-    count = out_ref.shape[1]
-    start = (1 - core if swapped else core) * (BLOCKS * BS - count)
-    cols = pl.ds(pl.multiple_of(start, BS), count)
-    move = pltpu.make_async_copy(g_ref.at[:, cols], out_ref, sem)
-    move.start()
-    move.wait()
-
-
-def cut(name, g, blocks, swapped):
+    start = (1 - core if swapped else core) * (BLOCKS * BS - count * len(outs))
+    moves = []
+    for i, out_ref in enumerate(outs):
+        cols = pl.ds(pl.multiple_of(start + i * count, HALF), count)
+        moves.append(pltpu.make_async_copy(g_ref.at[:, cols], out_ref, sems.at[i]))
+    for move in moves:
+        move.start()
+    for move in moves:
+        move.wait()
+
+
+def cut(name, g, columns, pieces, swapped):
+    out = jax.ShapeDtypeStruct((g.shape[0], columns // pieces), g.dtype)
     return pl.pallas_call(
         functools.partial(cut_kernel, swapped=swapped),
         in_specs=[ANY],
-        out_specs=VMEM,
-        out_shape=jax.ShapeDtypeStruct((g.shape[0], blocks * BS), g.dtype),
-        scratch_shapes=[pltpu.SemaphoreType.DMA(())],
+        out_specs=[VMEM] * pieces,
+        out_shape=[out] * pieces,
+        scratch_shapes=[pltpu.SemaphoreType.DMA((pieces,))],
         compiler_params=pltpu.CompilerParams(vmem_limit_bytes=52 * MIB),
         cost_estimate=pl.CostEstimate(flops=0, bytes_accessed=1000, transcendentals=0),
         name=name,
@@ -128,7 +135,7 @@
         ],
         compiler_params=pltpu.CompilerParams(vmem_limit_bytes=44 * MIB),
         cost_estimate=pl.CostEstimate(
-            flops=100_000_000_000, bytes_accessed=1000, transcendentals=0
+            flops=50_000_000_000, bytes_accessed=1000, transcendentals=0
         ),
         name="local_tiles",
     )(flags, g)
@@ -186,8 +193,8 @@
     )(keep, got)
 
 
-def sum_kernel(came_ref, wide_ref, part_ref, mask_ref, sum_ref, send_ref):
-    total = part_ref[...] + lax.dot_general(
+def sum_kernel(came_ref, wide_ref, part_ref, mask_ref, sum_ref, send_ref, *, half):
+    total = part_ref[half * HALF:(half + 1) * HALF] + lax.dot_general(
         came_ref[...], wide_ref[...], OVER_ROWS, preferred_element_type=jnp.float32
     )
     first = lax.axis_index("aux") == 0
@@ -195,39 +202,41 @@
     other_pair = jnp.where(first, 1.0, mask_ref[2:3, :])
     left = jnp.where(other_pair > 0, total[:, :BS], 0.0)
     right = jnp.where(near > 0, total[:, BS:], 0.0)
-    send_ref[:BS] = jnp.where(first, right, left)
-    send_ref[BS:] = jnp.where(first, 0.0, mask_ref[...])
+    send_ref[:HALF] = jnp.where(first, right, left)
+    send_ref[HALF:] = jnp.where(first, 0.0, mask_ref[...])
     sum_ref[:BS] = left.T
     sum_ref[BS:] = right.T
 
 
-def edge_sum(came, wide, part, mask):
-    return pl.pallas_call(
-        sum_kernel,
+def edge_sum(half, came, wide, part, mask):
+    return pl.pallas_call(
+        functools.partial(sum_kernel, half=half),
         in_specs=[VMEM] * 4,
         out_specs=[VMEM, VMEM],
         out_shape=[
-            jax.ShapeDtypeStruct((2 * BS, BS), jnp.float32),
-            jax.ShapeDtypeStruct((BS + 8, BS), jnp.float32),
+            jax.ShapeDtypeStruct((2 * BS, HALF), jnp.float32),
+            jax.ShapeDtypeStruct((HALF + 8, BS), jnp.float32),
         ],
         compiler_params=pltpu.CompilerParams(vmem_limit_bytes=16 * MIB),
         cost_estimate=pl.CostEstimate(
-            flops=50_000_000_000, bytes_accessed=1000, transcendentals=0
+            flops=half * 50_000_000_000, bytes_accessed=1000, transcendentals=0
         ),
         name="edge_sum",
     )(came, wide, part, mask)
 
 
-def finish_kernel(sum_ref, cross_ref, mask_ref, _, __, upper_ref, lower_ref, *scratch):
+def finish_kernel(sum_a, sum_b, cross_a, cross_b, mask_ref, _, __, upper_ref, lower_ref, *scratch):
     stages, sems = scratch[:3], scratch[3]
     core = lax.axis_index("aux")
     first = core == 0
-    near = jnp.where(first, cross_ref[BS:BS + 1, :], 1.0)
-    far = jnp.where(first, cross_ref[BS + 1:BS + 2, :], 1.0)
-    third = jnp.where(first, cross_ref[BS + 2:BS + 3, :], mask_ref[1:2, :])
-    stages[0][...] = jnp.where(near > 0, sum_ref[:BS], 0.0)
-    stages[1][...] = jnp.where(far > 0, sum_ref[BS:], 0.0)
-    stages[2][...] = jnp.where(third > 0, cross_ref[:BS], 0.0)
+    near = jnp.where(first, cross_a[HALF:HALF + 1, :HALF], 1.0)
+    far = jnp.where(first, cross_a[HALF + 1:HALF + 2, :HALF], 1.0)
+    third = jnp.where(first, cross_a[HALF + 2:HALF + 3, :], mask_ref[1:2, :])
+    for half, (sum_ref, cross_ref) in enumerate(((sum_a, cross_a), (sum_b, cross_b))):
+        rows = slice(half * HALF, (half + 1) * HALF)
+        stages[0][:, rows] = jnp.where(near > 0, sum_ref[:BS], 0.0)
+        stages[1][:, rows] = jnp.where(far > 0, sum_ref[BS:], 0.0)
+        stages[2][rows, :] = jnp.where(third > 0, cross_ref[:HALF], 0.0)
 
     def copies(band, places):
         moves = [
@@ -250,21 +259,21 @@
         copies(upper_ref, ((1, 2), (2, 1), (2, 2)))
 
 
-def finish(total, crossed, mask, upper, lower):
+def finish(sums, crossed, mask, upper, lower):
     return pl.pallas_call(
         finish_kernel,
-        in_specs=[VMEM, VMEM, VMEM, ANY, ANY],
+        in_specs=[VMEM] * 5 + [ANY, ANY],
         out_specs=[ANY, ANY],
         out_shape=[
             jax.ShapeDtypeStruct(upper.shape, upper.dtype),
             jax.ShapeDtypeStruct(lower.shape, lower.dtype),
         ],
-        input_output_aliases={3: 0, 4: 1},
+        input_output_aliases={5: 0, 6: 1},
         scratch_shapes=[pltpu.VMEM((BS, BS), jnp.float32)] * 3
         + [pltpu.SemaphoreType.DMA((3,))],
         compiler_params=pltpu.CompilerParams(vmem_limit_bytes=8 * MIB),
         name="finish",
-    )(total, crossed, mask, upper, lower)
+    )(*sums, *crossed, mask, upper, lower)
 
 
 def body(factors, pair_keep):
@@ -280,16 +289,19 @@
 
     g = jnp.swapaxes(factors[0], 0, 1)
     flags = jnp.swapaxes(pair_keep, 0, 1)
-    came_one = lax.ppermute(cut("cut_first", g, 1, True), axes, along)
-    came_two = lax.ppermute(cut("cut_second", g, 1, False), axes, cross)
-    other = lax.ppermute(cut("cut_wide", g, 2, True), axes, swap)
+    came_one = lax.ppermute(cut("cut_first", g, BS, 1, True)[0], axes, along)
+    came_two = [lax.ppermute(piece, axes, cross) for piece in cut("cut_second", g, BS, 2, False)]
+    other = lax.ppermute(cut("cut_wide", g, 2 * BS, 1, True)[0], axes, swap)
     keep, give, mask, wide = local_tiles(flags, g)
     got = lax.ppermute(give, axes, swap)
     part = edge_partial(came_one, wide)
-    total, send = edge_sum(came_two, other, part, mask)
-    crossed = lax.ppermute(send, axes, cross)
+    sums, crossed = [], []
+    for half, came in enumerate(came_two):
+        total, send = edge_sum(half, came, other, part, mask)
+        sums.append(total)
+        crossed.append(lax.ppermute(send, axes, cross))
     upper, lower = local_bands(keep, got)
-    return tuple(finish(total, crossed, mask, upper, lower))
+    return tuple(finish(sums, crossed, mask, upper, lower))
 
 
 def solution(mesh):

time: 57.6 us -> 55.8 us (0.969)
  waiting for transfers between devices: 21.3 us -> 6.41 us
  starting transfers between devices: 13.7 us -> 26.5 us
    ppermute x4 -> x6, waiting for transfers between devices: 21.3 us -> 6.41 us  [the longest x1 3.39 us: body(): came_one = lax.ppermute(cut('cut_first', g, BS, 1, True)[0], axes, along)]
    ppermute x4 -> x6, starting transfers between devices: 13.6 us -> 26.4 us  [the longest x2 12.1 us: body(): crossed.append(lax.ppermute(send, axes, cross))]
    pallas_call x2 -> x3, Pallas kernels: 2.07 us -> 2.33 us  [the longest x2 1.39 us: edge_sum(): pl.pallas_call(functools.partial(sum_kernel, half=half), in_specs=[VMEM]...]
  transfers between devices with their start and end apart: 5 -> 7, of which waited for: 3 -> 4; matrix products, arithmetic and copies ran while one was open for 0% -> 0% of each run, Pallas kernels for 34% -> 35%
where the time goes in v5:
time: 55.8 us; the launch traced here: 55.6 us
  starting transfers between devices  26.5 us (47%)
  Pallas kernels  22 us (39%)
  waiting for transfers between devices  6.41 us (11%)
  between operations  0.71 us (1%)
    ppermute x2, starting transfers between devices, body(): crossed.append(lax.ppermute(send, axes, cross))  12.1 us
    pallas_call x1, Pallas kernels, local_tiles(): pl.pallas_call(local_kernel, in_specs=[SMEM, ANY], out_specs=[VMEM, VMEM,...  9.98 us
    ppermute x1, starting transfers between devices, body(): other = lax.ppermute(cut('cut_wide', g, 2 * BS, 1, True)[0], axes, swap)  6.63 us
    pallas_call x3, Pallas kernels, cut(): pl.pallas_call(functools.partial(cut_kernel, swapped=swapped), in_specs=[...  6.3 us
    ppermute x2, starting transfers between devices, body(): lax.ppermute(piece, axes, cross)  6.05 us
    ppermute x1, waiting for transfers between devices, body(): came_one = lax.ppermute(cut('cut_first', g, BS, 1, True)[0], axes, along)  3.39 us
    pallas_call x1, Pallas kernels, local_bands(): pl.pallas_call(band_kernel, in_specs=[VMEM, VMEM], out_specs=[VMEM, VMEM]...  2.36 us
    ppermute x2, waiting for transfers between devices, body(): crossed.append(lax.ppermute(send, axes, cross))  1.8 us
  transfers between devices with their start and end apart: 7, of which 4 were waited for; matrix products, arithmetic and copies ran while one was open for 0% of the time, Pallas kernels for 35%

profile of v5, /device:TPU:6, one launch (start us, length us, event | category | flops | bytes accessed | tf_op | source)
XLA Modules:
  0.0 55.6 jit_solution(8311201810950726451)
XLA Ops:
  0.6 1.4 %cut_first.1 = bf16[3000,256]{1,0:T(8,128)(2,1)S(1)} custom-call(bf16[3000,1536]{1,0:T(8,128)(2,1)} %bitcast.5), custom_call_target="tpu_custom_call" | custom-call | bytes 1000 | tf_op jit(solution)/shard_map/cut_first/pallas_call | solution.py:44
  2.0 1.7 %collective-permute-start.2 = (bf16[3000,256]{1,0:T(8,128)(2,1)S(1)}, bf16[3000,256]{1,0:T(8,128)(2,1)S(1)}, u32[]{:S(2)}, u32[]{:S(2)}) collective-permute-start(bf16[3000,256]{1,0:T(8,128)(2,1)S(1)} %cut_first.1), channel_id=1, source_target_pairs={{0,2},{2,4},{4,6},{6,8},{8,10},{10,12},{12,14},{14,16},{16,18},{18... | collective-permute-start | bytes 4608008 | tf_op jit(solution)/shard_map/ppermute | solution.py:292
  3.7 3.5 %cut_wide.1 = bf16[3000,512]{1,0:T(8,128)(2,1)} custom-call(bf16[3000,1536]{1,0:T(8,128)(2,1)} %bitcast.6), custom_call_target="tpu_custom_call" | custom-call | bytes 1000 | tf_op jit(solution)/shard_map/cut_wide/pallas_call | solution.py:44
  7.2 0.0 copy-start
  7.2 6.6 %collective-permute-start.1 = (bf16[3000,512]{1,0:T(8,128)(2,1)}, bf16[3000,512]{1,0:T(8,128)(2,1)S(1)}, u32[]{:S(2)}, u32[]{:S(2)}) collective-permute-start(bf16[3000,512]{1,0:T(8,128)(2,1)} %cut_wide.1), channel_id=1, source_target_pairs={{0,1},{1,0},{2,3},{3,2},{4,5},{5,4},{6,7},{7,6},{8,9},{9,8},{10,11... | collective-permute-start | bytes 9216008 | tf_op jit(solution)/shard_map/ppermute | solution.py:294
  13.9 1.4 %cut_second.1 = (bf16[3000,128]{1,0:T(8,128)(2,1)S(1)}, bf16[3000,128]{1,0:T(8,128)(2,1)S(1)}) custom-call(bf16[3000,1536]{1,0:T(8,128)(2,1)} %bitcast.7), custom_call_target="tpu_custom_call" | custom-call | bytes 1000 | tf_op jit(solution)/shard_map/cut_second/pallas_call | solution.py:44
  15.3 0.7 %collective-permute-start.3 = (bf16[3000,128]{1,0:T(8,128)(2,1)S(1)}, bf16[3000,128]{1,0:T(8,128)(2,1)S(1)}, u32[]{:S(2)}, u32[]{:S(2)}) collective-permute-start(bf16[3000,128]{1,0:T(8,128)(2,1)S(1)} %get-tuple-element.18), channel_id=1, source_target_pairs={{1,2},{3,4},{5,6},{7,8},{9,10},{11,12},{13,14},{15,16},{17,18},{19... | collective-permute-start | bytes 2304008 | tf_op jit(solution)/shard_map/ppermute | solution.py:293
  15.9 5.4 %collective-permute-start = (bf16[3000,128]{1,0:T(8,128)(2,1)S(1)}, bf16[3000,128]{1,0:T(8,128)(2,1)S(1)}, u32[]{:S(2)}, u32[]{:S(2)}) collective-permute-start(bf16[3000,128]{1,0:T(8,128)(2,1)S(1)} %get-tuple-element.14), channel_id=1, source_target_pairs={{1,2},{3,4},{5,6},{7,8},{9,10},{11,12},{13,14},{15,16},{17,18},{19... | collective-permute-start | bytes 2304008 | tf_op jit(solution)/shard_map/ppermute | solution.py:293
  21.3 10.0 %local_tiles.1 = (f32[9,256,256]{2,1,0:T(8,128)S(1)}, f32[9,256,256]{2,1,0:T(8,128)S(1)}, f32[8,256]{1,0:T(8,128)S(1)}, bf16[3000,512]{1,0:T(8,128)(2,1)S(1)}) custom-call(s32[2,6]{1,0:T(2,128)S(1)} %bitcast.4, bf16[3000,1536]{1,0:T(8,128)(2,1)} %bitcast.8), custom_call_target="tpu_custom_call" | custom-call | flops 49999998976 | bytes 1000 | tf_op jit(solution)/shard_map/local_tiles/pallas_call | solution.py:122
  31.3 0.1 collective-permute-start.6
  31.4 3.4 %collective-permute-done.2.came_ref = bf16[3000,256]{1,0:T(8,128)(2,1)S(1)} collective-permute-done((bf16[3000,256]{1,0:T(8,128)(2,1)S(1)}, bf16[3000,256]{1,0:T(8,128)(2,1)S(1)}, u32[]{:S(2)}, u32[]{:S(2)}) %collective-permute-start.2) | collective-permute-done | bytes 1536032 | tf_op jit(solution)/shard_map/ppermute | solution.py:292
  34.8 1.0 %edge_partial.1.part_ref = f32[256,512]{1,0:T(8,128)S(1)} custom-call(bf16[3000,256]{1,0:T(8,128)(2,1)S(1)} %collective-permute-done.2.came_ref, bf16[3000,512]{1,0:T(8,128)(2,1)S(1)} %get-tuple-element.15.wide_ref), custom_call_target="tpu_custom_call" | custom-call | bytes 1000 | tf_op jit(solution)/shard_map/edge_partial/pallas_call | solution.py:151
  35.8 1.1 %collective-permute-done.3.came_ref = bf16[3000,128]{1,0:T(8,128)(2,1)S(1)} collective-permute-done((bf16[3000,128]{1,0:T(8,128)(2,1)S(1)}, bf16[3000,128]{1,0:T(8,128)(2,1)S(1)}, u32[]{:S(2)}, u32[]{:S(2)}) %collective-permute-start.3) | collective-permute-done | bytes 768032 | tf_op jit(solution)/shard_map/ppermute | solution.py:293
  36.9 0.0 collective-permute-done.1.wide_ref
  36.9 0.7 %edge_sum.3 = (f32[512,128]{1,0:T(8,128)S(1)}, f32[136,256]{1,0:T(8,128)S(1)}) custom-call(bf16[3000,128]{1,0:T(8,128)(2,1)S(1)} %collective-permute-done.3.came_ref, bf16[3000,512]{1,0:T(8,128)(2,1)S(1)} %collective-permute-done.1.wide_ref, f32[256,512]{1,0:T(8,128)S(1)} %edge_partial.1.part_ref, f32[8,256]{1,0:T(8,128)S(1)} %get-tuple-element.16.mask_ref), custom_call_target="tpu_custom_call" | custom-call | flops 49999998976 | bytes 1000 | tf_op jit(solution)/shard_map/edge_sum/pallas_call | solution.py:212
  37.6 7.4 %collective-permute-start.5 = (f32[136,256]{1,0:T(8,128)S(1)}, f32[136,256]{1,0:T(8,128)S(1)}, u32[]{:S(2)}, u32[]{:S(2)}) collective-permute-start(f32[136,256]{1,0:T(8,128)S(1)} %get-tuple-element.21), channel_id=1, source_target_pairs={{1,2},{3,4},{5,6},{7,8},{9,10},{11,12},{13,14},{15,16},{17,18},{19... | collective-permute-start | bytes 417800 | tf_op jit(solution)/shard_map/ppermute | solution.py:302
  45.1 0.1 collective-permute-done.came_ref
  45.2 0.7 %edge_sum.2 = (f32[512,128]{1,0:T(8,128)S(1)}, f32[136,256]{1,0:T(8,128)S(1)}) custom-call(bf16[3000,128]{1,0:T(8,128)(2,1)S(1)} %collective-permute-done.came_ref, bf16[3000,512]{1,0:T(8,128)(2,1)S(1)} %collective-permute-done.1.wide_ref, f32[256,512]{1,0:T(8,128)S(1)} %edge_partial.1.part_ref, f32[8,256]{1,0:T(8,128)S(1)} %get-tuple-element.16.mask_ref), custom_call_target="tpu_custom_call" | custom-call | bytes 1000 | tf_op jit(solution)/shard_map/edge_sum/pallas_call | solution.py:212
  45.9 4.6 %collective-permute-start.4 = (f32[136,256]{1,0:T(8,128)S(1)}, f32[136,256]{1,0:T(8,128)S(1)}, u32[]{:S(2)}, u32[]{:S(2)}) collective-permute-start(f32[136,256]{1,0:T(8,128)S(1)} %get-tuple-element.20), channel_id=1, source_target_pairs={{1,2},{3,4},{5,6},{7,8},{9,10},{11,12},{13,14},{15,16},{17,18},{19... | collective-permute-start | bytes 417800 | tf_op jit(solution)/shard_map/ppermute | solution.py:302
  50.5 0.0 collective-permute-done.6.got_ref
  50.5 2.4 %local_bands.1 = (f32[768,768]{1,0:T(8,128)}, f32[768,512]{1,0:T(8,128)}) custom-call(f32[9,256,256]{2,1,0:T(8,128)S(1)} %get-tuple-element.22.keep_ref, f32[9,256,256]{2,1,0:T(8,128)S(1)} %collective-permute-done.6.got_ref), custom_call_target="tpu_custom_call" | custom-call | flops 10000000 | bytes 12000000 | tf_op jit(solution)/shard_map/local_bands/pallas_call | solution.py:180
  52.8 0.0 collective-permute-done.5.cross_b
  52.9 1.8 %collective-permute-done.4.cross_a = f32[136,256]{1,0:T(8,128)S(1)} collective-permute-done((f32[136,256]{1,0:T(8,128)S(1)}, f32[136,256]{1,0:T(8,128)S(1)}, u32[]{:S(2)}, u32[]{:S(2)}) %collective-permute-start.4) | collective-permute-done | bytes 139296 | tf_op jit(solution)/shard_map/ppermute | solution.py:302
  54.7 0.9 %finish.1 = (f32[768,768]{1,0:T(8,128)}, f32[768,512]{1,0:T(8,128)}) custom-call(f32[512,128]{1,0:T(8,128)S(1)} %get-tuple-element.17.sum_a, f32[512,128]{1,0:T(8,128)S(1)} %get-tuple-element.19.sum_b, f32[136,256]{1,0:T(8,128)S(1)} %collective-permute-done.4.cross_a, ...), custom_call_target="tpu_custom_call", output_to_operand_aliasing={{0}: (5, {}), {1}: (6, {})} | custom-call | tf_op jit(solution)/shard_map/finish/pallas_call | solution.py:263
  (1 shorter events, 0.0 us)
Async XLA Ops:
  2.0 32.7 %collective-permute-start.2 = (bf16[3000,256]{1,0:T(8,128)(2,1)S(1)}, bf16[3000,256]{1,0:T(8,128)(2,1)S(1)}, u32[]{:S(2)}, u32[]{:S(2)}) collective-permute-start(bf16[3000,256]{1,0:T(8,128)(2,1)S(1)} %cut_first.1), channel_id=1, source_target_pairs={{0,2},{2,4},{4,6},{6,8},{8,10},{10,12},{12,14},{14,16},{16,18},{18... | collective-permute-start | bytes 4608008 | tf_op jit(solution)/shard_map/ppermute | solution.py:292
  7.2 14.1 %copy-start = (s32[6,2]{0,1:T(2,128)S(1)}, s32[6,2]{0,1:T(2,128)}, u32[]{:S(2)}) copy-start(s32[6,2]{0,1:T(2,128)} %param.3) | copy-start | bytes 148
  7.2 29.7 %collective-permute-start.1 = (bf16[3000,512]{1,0:T(8,128)(2,1)}, bf16[3000,512]{1,0:T(8,128)(2,1)S(1)}, u32[]{:S(2)}, u32[]{:S(2)}) collective-permute-start(bf16[3000,512]{1,0:T(8,128)(2,1)} %cut_wide.1), channel_id=1, source_target_pairs={{0,1},{1,0},{2,3},{3,2},{4,5},{5,4},{6,7},{7,6},{8,9},{9,8},{10,11... | collective-permute-start | bytes 9216008 | tf_op jit(solution)/shard_map/ppermute | solution.py:294
  15.3 21.7 %collective-permute-start.3 = (bf16[3000,128]{1,0:T(8,128)(2,1)S(1)}, bf16[3000,128]{1,0:T(8,128)(2,1)S(1)}, u32[]{:S(2)}, u32[]{:S(2)}) collective-permute-start(bf16[3000,128]{1,0:T(8,128)(2,1)S(1)} %get-tuple-element.18), channel_id=1, source_target_pairs={{1,2},{3,4},{5,6},{7,8},{9,10},{11,12},{13,14},{15,16},{17,18},{19... | collective-permute-start | bytes 2304008 | tf_op jit(solution)/shard_map/ppermute | solution.py:293
  15.9 29.2 %collective-permute-start = (bf16[3000,128]{1,0:T(8,128)(2,1)S(1)}, bf16[3000,128]{1,0:T(8,128)(2,1)S(1)}, u32[]{:S(2)}, u32[]{:S(2)}) collective-permute-start(bf16[3000,128]{1,0:T(8,128)(2,1)S(1)} %get-tuple-element.14), channel_id=1, source_target_pairs={{1,2},{3,4},{5,6},{7,8},{9,10},{11,12},{13,14},{15,16},{17,18},{19... | collective-permute-start | bytes 2304008 | tf_op jit(solution)/shard_map/ppermute | solution.py:293
  31.3 19.2 %collective-permute-start.6 = (f32[9,256,256]{2,1,0:T(8,128)S(1)}, f32[9,256,256]{2,1,0:T(8,128)S(1)}, u32[]{:S(2)}, u32[]{:S(2)}) collective-permute-start(f32[9,256,256]{2,1,0:T(8,128)S(1)} %get-tuple-element.23), channel_id=1, source_target_pairs={{0,1},{1,0},{2,3},{3,2},{4,5},{5,4},{6,7},{7,6},{8,9},{9,8},{10,11... | collective-permute-start | bytes 7077896 | tf_op jit(solution)/shard_map/ppermute | solution.py:296
  37.6 15.2 %collective-permute-start.5 = (f32[136,256]{1,0:T(8,128)S(1)}, f32[136,256]{1,0:T(8,128)S(1)}, u32[]{:S(2)}, u32[]{:S(2)}) collective-permute-start(f32[136,256]{1,0:T(8,128)S(1)} %get-tuple-element.21), channel_id=1, source_target_pairs={{1,2},{3,4},{5,6},{7,8},{9,10},{11,12},{13,14},{15,16},{17,18},{19... | collective-permute-start | bytes 417800 | tf_op jit(solution)/shard_map/ppermute | solution.py:302
  45.9 8.8 %collective-permute-start.4 = (f32[136,256]{1,0:T(8,128)S(1)}, f32[136,256]{1,0:T(8,128)S(1)}, u32[]{:S(2)}, u32[]{:S(2)}) collective-permute-start(f32[136,256]{1,0:T(8,128)S(1)} %get-tuple-element.20), channel_id=1, source_target_pairs={{1,2},{3,4},{5,6},{7,8},{9,10},{11,12},{13,14},{15,16},{17,18},{19... | collective-permute-start | bytes 417800 | tf_op jit(solution)/shard_map/ppermute | solution.py:302

commit v6 on v5

--- a/solution.py
+++ b/solution.py
@@ -11,6 +11,7 @@
 BLOCKS = 6
 HELD = 3
 HALF = 128
+HEAD = 512
 SLOTS = HELD * HELD
 MIB = 1024 * 1024
 
@@ -24,25 +25,25 @@
 OVER_ROWS = (((0,), (0,)), ((), ()))
 
 
-def cut_kernel(g_ref, *refs, swapped):
+def cut_kernel(g_ref, *refs, swapped, skip):
     outs, sems = refs[:-1], refs[-1]
-    count = outs[0].shape[1]
+    rows, count = outs[0].shape
     core = lax.axis_index("aux")
     start = (1 - core if swapped else core) * (BLOCKS * BS - count * len(outs))
     moves = []
     for i, out_ref in enumerate(outs):
         cols = pl.ds(pl.multiple_of(start + i * count, HALF), count)
-        moves.append(pltpu.make_async_copy(g_ref.at[:, cols], out_ref, sems.at[i]))
+        moves.append(pltpu.make_async_copy(g_ref.at[pl.ds(skip, rows), cols], out_ref, sems.at[i]))
     for move in moves:
         move.start()
     for move in moves:
         move.wait()
 
 
-def cut(name, g, columns, pieces, swapped):
-    out = jax.ShapeDtypeStruct((g.shape[0], columns // pieces), g.dtype)
-    return pl.pallas_call(
-        functools.partial(cut_kernel, swapped=swapped),
+def cut(name, g, columns, pieces, swapped, rows=None, skip=0):
+    out = jax.ShapeDtypeStruct((rows or g.shape[0], columns // pieces), g.dtype)
+    return pl.pallas_call(
+        functools.partial(cut_kernel, swapped=swapped, skip=skip),
         in_specs=[ANY],
         out_specs=[VMEM] * pieces,
         out_shape=[out] * pieces,
@@ -141,22 +142,28 @@
     )(flags, g)
 
 
-def edge_kernel(came_ref, wide_ref, part_ref):
-    part_ref[...] = lax.dot_general(
-        came_ref[...], wide_ref[...], OVER_ROWS, preferred_element_type=jnp.float32
-    )
-
-
-def edge_partial(came, wide):
-    return pl.pallas_call(
-        edge_kernel,
-        in_specs=[VMEM, VMEM],
+def over_rows(left, right):
+    return lax.dot_general(left, right, OVER_ROWS, preferred_element_type=jnp.float32)
+
+
+def head_kernel(head_ref, wide_ref, part_ref):
+    part_ref[...] = over_rows(head_ref[...], wide_ref[:HEAD])
+
+
+def rest_kernel(rest_ref, wide_ref, head_ref, part_ref):
+    part_ref[...] = head_ref[...] + over_rows(rest_ref[...], wide_ref[HEAD:])
+
+
+def edge_partial(name, kernel, *args):
+    return pl.pallas_call(
+        kernel,
+        in_specs=[VMEM] * len(args),
         out_specs=VMEM,
         out_shape=jax.ShapeDtypeStruct((BS, 2 * BS), jnp.float32),
         compiler_params=pltpu.CompilerParams(vmem_limit_bytes=16 * MIB),
         cost_estimate=pl.CostEstimate(flops=0, bytes_accessed=1000, transcendentals=0),
-        name="edge_partial",
-    )(came, wide)
+        name=name,
+    )(*args)
 
 
 def band_kernel(keep_ref, got_ref, upper_ref, lower_ref):
@@ -194,9 +201,7 @@
 
 
 def sum_kernel(came_ref, wide_ref, part_ref, mask_ref, sum_ref, send_ref, *, half):
-    total = part_ref[half * HALF:(half + 1) * HALF] + lax.dot_general(
-        came_ref[...], wide_ref[...], OVER_ROWS, preferred_element_type=jnp.float32
-    )
+    total = part_ref[half * HALF:(half + 1) * HALF] + over_rows(came_ref[...], wide_ref[...])
     first = lax.axis_index("aux") == 0
     near = jnp.where(first, 1.0, mask_ref[0:1, :])
     other_pair = jnp.where(first, 1.0, mask_ref[2:3, :])
@@ -289,12 +294,15 @@
 
     g = jnp.swapaxes(factors[0], 0, 1)
     flags = jnp.swapaxes(pair_keep, 0, 1)
-    came_one = lax.ppermute(cut("cut_first", g, BS, 1, True)[0], axes, along)
+    nocc = g.shape[0]
+    head = lax.ppermute(cut("cut_head", g, BS, 1, True, HEAD)[0], axes, along)
+    rest = lax.ppermute(cut("cut_rest", g, BS, 1, True, nocc - HEAD, HEAD)[0], axes, along)
     came_two = [lax.ppermute(piece, axes, cross) for piece in cut("cut_second", g, BS, 2, False)]
     other = lax.ppermute(cut("cut_wide", g, 2 * BS, 1, True)[0], axes, swap)
     keep, give, mask, wide = local_tiles(flags, g)
     got = lax.ppermute(give, axes, swap)
-    part = edge_partial(came_one, wide)
+    part = edge_partial("edge_head", head_kernel, head, wide)
+    part = edge_partial("edge_rest", rest_kernel, rest, wide, part)
     sums, crossed = [], []
     for half, came in enumerate(came_two):
         total, send = edge_sum(half, came, other, part, mask)

time: 55.8 us -> 55.4 us (level)
  Pallas kernels: 22 us -> 23 us
  starting transfers between devices: 26.5 us -> 25.5 us
    ppermute x1 -> x2, waiting for transfers between devices: 3.39 us -> 0.01 us  [the longest x1 0.01 us: body(): head = lax.ppermute(cut('cut_head', g, BS, 1, True, HEAD)[0], axes, along)]
    ppermute x2, waiting for transfers between devices: 1.22 us -> 4.08 us  [body(): lax.ppermute(piece, axes, cross)]
    ppermute x1 -> x2, starting transfers between devices: 1.66 us -> 3.31 us  [the longest x1 1.66 us: body(): head = lax.ppermute(cut('cut_head', g, BS, 1, True, HEAD)[0], axes, along)]
    ppermute x2, starting transfers between devices: 12.1 us -> 10.5 us  [body(): crossed.append(lax.ppermute(send, axes, cross))]
    ppermute x1, starting transfers between devices: 6.63 us -> 5.52 us  [body(): other = lax.ppermute(cut('cut_wide', g, 2 * BS, 1, True)[0], axes, swap)]
    pallas_call x4 -> x6, Pallas kernels: 7.3 us -> 8.34 us  [the longest x4 7.16 us: cut(): pl.pallas_call(functools.partial(cut_kernel, swapped=swapped, skip=skip),...]
  transfers between devices with their start and end apart: 7 -> 8, of which waited for: 4 -> 3; matrix products, arithmetic and copies ran while one was open for 0% -> 0% of each run, Pallas kernels for 35% -> 38%
where the time goes in v6:
time: 55.4 us; the launch traced here: 55.1 us
  starting transfers between devices  25.5 us (46%)
  Pallas kernels  23 us (42%)
  waiting for transfers between devices  5.89 us (11%)
  between operations  0.74 us (1%)
    ppermute x2, starting transfers between devices, body(): crossed.append(lax.ppermute(send, axes, cross))  10.5 us
    pallas_call x1, Pallas kernels, local_tiles(): pl.pallas_call(local_kernel, in_specs=[SMEM, ANY], out_specs=[VMEM, VMEM,...  9.98 us
    pallas_call x4, Pallas kernels, cut(): pl.pallas_call(functools.partial(cut_kernel, swapped=swapped, skip=skip),...  7.16 us
    ppermute x2, starting transfers between devices, body(): lax.ppermute(piece, axes, cross)  6.05 us
    ppermute x1, starting transfers between devices, body(): other = lax.ppermute(cut('cut_wide', g, 2 * BS, 1, True)[0], axes, swap)  5.52 us
    ppermute x2, waiting for transfers between devices, body(): lax.ppermute(piece, axes, cross)  4.08 us
    pallas_call x1, Pallas kernels, local_bands(): pl.pallas_call(band_kernel, in_specs=[VMEM, VMEM], out_specs=[VMEM, VMEM]...  2.36 us
    ppermute x2, waiting for transfers between devices, body(): crossed.append(lax.ppermute(send, axes, cross))  1.81 us
  transfers between devices with their start and end apart: 8, of which 3 were waited for; matrix products, arithmetic and copies ran while one was open for 0% of the time, Pallas kernels for 38%

profile of v6, /device:TPU:6, one launch (start us, length us, event | category | flops | bytes accessed | tf_op | source)
XLA Modules:
  0.0 55.1 jit_solution(6461158398046837984)
XLA Ops:
  0.6 1.0 %cut_head.1 = bf16[512,256]{1,0:T(8,128)(2,1)S(1)} custom-call(bf16[3000,1536]{1,0:T(8,128)(2,1)} %bitcast.5), custom_call_target="tpu_custom_call" | custom-call | bytes 1000 | tf_op jit(solution)/shard_map/cut_head/pallas_call | solution.py:45
  1.6 1.7 %collective-permute-start.3 = (bf16[512,256]{1,0:T(8,128)(2,1)S(1)}, bf16[512,256]{1,0:T(8,128)(2,1)S(1)}, u32[]{:S(2)}, u32[]{:S(2)}) collective-permute-start(bf16[512,256]{1,0:T(8,128)(2,1)S(1)} %cut_head.1), channel_id=1, source_target_pairs={{0,2},{2,4},{4,6},{6,8},{8,10},{10,12},{12,14},{14,16},{16,18},{18... | collective-permute-start | bytes 786440 | tf_op jit(solution)/shard_map/ppermute | solution.py:298
  3.3 1.3 %cut_rest.1 = bf16[2488,256]{1,0:T(8,128)(2,1)S(1)} custom-call(bf16[3000,1536]{1,0:T(8,128)(2,1)} %bitcast.6), custom_call_target="tpu_custom_call" | custom-call | bytes 1000 | tf_op jit(solution)/shard_map/cut_rest/pallas_call | solution.py:45
  4.6 1.7 %collective-permute-start.2 = (bf16[2488,256]{1,0:T(8,128)(2,1)S(1)}, bf16[2488,256]{1,0:T(8,128)(2,1)S(1)}, u32[]{:S(2)}, u32[]{:S(2)}) collective-permute-start(bf16[2488,256]{1,0:T(8,128)(2,1)S(1)} %cut_rest.1), channel_id=1, source_target_pairs={{0,2},{2,4},{4,6},{6,8},{8,10},{10,12},{12,14},{14,16},{16,18},{18... | collective-permute-start | bytes 3821576 | tf_op jit(solution)/shard_map/ppermute | solution.py:299
  6.2 3.5 %cut_wide.1 = bf16[3000,512]{1,0:T(8,128)(2,1)} custom-call(bf16[3000,1536]{1,0:T(8,128)(2,1)} %bitcast.7), custom_call_target="tpu_custom_call" | custom-call | bytes 1000 | tf_op jit(solution)/shard_map/cut_wide/pallas_call | solution.py:45
  9.7 0.0 copy-start
  9.7 5.5 %collective-permute-start.1 = (bf16[3000,512]{1,0:T(8,128)(2,1)}, bf16[3000,512]{1,0:T(8,128)(2,1)S(1)}, u32[]{:S(2)}, u32[]{:S(2)}) collective-permute-start(bf16[3000,512]{1,0:T(8,128)(2,1)} %cut_wide.1), channel_id=1, source_target_pairs={{0,1},{1,0},{2,3},{3,2},{4,5},{5,4},{6,7},{7,6},{8,9},{9,8},{10,11... | collective-permute-start | bytes 9216008 | tf_op jit(solution)/shard_map/ppermute | solution.py:301
  15.3 1.4 %cut_second.1 = (bf16[3000,128]{1,0:T(8,128)(2,1)S(1)}, bf16[3000,128]{1,0:T(8,128)(2,1)S(1)}) custom-call(bf16[3000,1536]{1,0:T(8,128)(2,1)} %bitcast.8), custom_call_target="tpu_custom_call" | custom-call | bytes 1000 | tf_op jit(solution)/shard_map/cut_second/pallas_call | solution.py:45
  16.7 0.2 collective-permute-start.4
  16.9 5.8 %collective-permute-start = (bf16[3000,128]{1,0:T(8,128)(2,1)S(1)}, bf16[3000,128]{1,0:T(8,128)(2,1)S(1)}, u32[]{:S(2)}, u32[]{:S(2)}) collective-permute-start(bf16[3000,128]{1,0:T(8,128)(2,1)S(1)} %get-tuple-element.14), channel_id=1, source_target_pairs={{1,2},{3,4},{5,6},{7,8},{9,10},{11,12},{13,14},{15,16},{17,18},{19... | collective-permute-start | bytes 2304008 | tf_op jit(solution)/shard_map/ppermute | solution.py:300
  22.7 10.0 %local_tiles.1 = (f32[9,256,256]{2,1,0:T(8,128)S(1)}, f32[9,256,256]{2,1,0:T(8,128)S(1)}, f32[8,256]{1,0:T(8,128)S(1)}, bf16[3000,512]{1,0:T(8,128)(2,1)S(1)}) custom-call(s32[2,6]{1,0:T(2,128)S(1)} %bitcast.4, bf16[3000,1536]{1,0:T(8,128)(2,1)} %bitcast.9), custom_call_target="tpu_custom_call" | custom-call | flops 49999998976 | bytes 1000 | tf_op jit(solution)/shard_map/local_tiles/pallas_call | solution.py:123
  32.7 0.0 collective-permute-done.3.head_ref
  32.7 0.1 collective-permute-start.7
  32.8 0.3 edge_head.1.head_ref
  33.1 0.9 %edge_rest.1.part_ref = f32[256,512]{1,0:T(8,128)S(1)} custom-call(bf16[2488,256]{1,0:T(8,128)(2,1)S(1)} %collective-permute-done.2.rest_ref, bf16[3000,512]{1,0:T(8,128)(2,1)S(1)} %get-tuple-element.15.wide_ref, f32[256,512]{1,0:T(8,128)S(1)} %edge_head.1.head_ref), custom_call_target="tpu_custom_call" | custom-call | bytes 1000 | tf_op jit(solution)/shard_map/edge_rest/pallas_call | solution.py:158
  34.0 2.5 %collective-permute-done.4.came_ref = bf16[3000,128]{1,0:T(8,128)(2,1)S(1)} collective-permute-done((bf16[3000,128]{1,0:T(8,128)(2,1)S(1)}, bf16[3000,128]{1,0:T(8,128)(2,1)S(1)}, u32[]{:S(2)}, u32[]{:S(2)}) %collective-permute-start.4) | collective-permute-done | bytes 768032 | tf_op jit(solution)/shard_map/ppermute | solution.py:300
  36.5 0.7 %edge_sum.3 = (f32[512,128]{1,0:T(8,128)S(1)}, f32[136,256]{1,0:T(8,128)S(1)}) custom-call(bf16[3000,128]{1,0:T(8,128)(2,1)S(1)} %collective-permute-done.4.came_ref, bf16[3000,512]{1,0:T(8,128)(2,1)S(1)} %collective-permute-done.1.wide_ref, f32[256,512]{1,0:T(8,128)S(1)} %edge_rest.1.part_ref, f32[8,256]{1,0:T(8,128)S(1)} %get-tuple-element.16.mask_ref), custom_call_target="tpu_custom_call" | custom-call | flops 49999998976 | bytes 1000 | tf_op jit(solution)/shard_map/edge_sum/pallas_call | solution.py:217
  37.2 5.9 %collective-permute-start.6 = (f32[136,256]{1,0:T(8,128)S(1)}, f32[136,256]{1,0:T(8,128)S(1)}, u32[]{:S(2)}, u32[]{:S(2)}) collective-permute-start(f32[136,256]{1,0:T(8,128)S(1)} %get-tuple-element.21), channel_id=1, source_target_pairs={{1,2},{3,4},{5,6},{7,8},{9,10},{11,12},{13,14},{15,16},{17,18},{19... | collective-permute-start | bytes 417800 | tf_op jit(solution)/shard_map/ppermute | solution.py:310
  43.1 1.6 %collective-permute-done.came_ref = bf16[3000,128]{1,0:T(8,128)(2,1)S(1)} collective-permute-done((bf16[3000,128]{1,0:T(8,128)(2,1)S(1)}, bf16[3000,128]{1,0:T(8,128)(2,1)S(1)}, u32[]{:S(2)}, u32[]{:S(2)}) %collective-permute-start) | collective-permute-done | bytes 768032 | tf_op jit(solution)/shard_map/ppermute | solution.py:300
  44.7 0.7 %edge_sum.2 = (f32[512,128]{1,0:T(8,128)S(1)}, f32[136,256]{1,0:T(8,128)S(1)}) custom-call(bf16[3000,128]{1,0:T(8,128)(2,1)S(1)} %collective-permute-done.came_ref, bf16[3000,512]{1,0:T(8,128)(2,1)S(1)} %collective-permute-done.1.wide_ref, f32[256,512]{1,0:T(8,128)S(1)} %edge_rest.1.part_ref, f32[8,256]{1,0:T(8,128)S(1)} %get-tuple-element.16.mask_ref), custom_call_target="tpu_custom_call" | custom-call | bytes 1000 | tf_op jit(solution)/shard_map/edge_sum/pallas_call | solution.py:217
  45.4 4.6 %collective-permute-start.5 = (f32[136,256]{1,0:T(8,128)S(1)}, f32[136,256]{1,0:T(8,128)S(1)}, u32[]{:S(2)}, u32[]{:S(2)}) collective-permute-start(f32[136,256]{1,0:T(8,128)S(1)} %get-tuple-element.20), channel_id=1, source_target_pairs={{1,2},{3,4},{5,6},{7,8},{9,10},{11,12},{13,14},{15,16},{17,18},{19... | collective-permute-start | bytes 417800 | tf_op jit(solution)/shard_map/ppermute | solution.py:310
  50.0 2.4 %local_bands.1 = (f32[768,768]{1,0:T(8,128)}, f32[768,512]{1,0:T(8,128)}) custom-call(f32[9,256,256]{2,1,0:T(8,128)S(1)} %get-tuple-element.22.keep_ref, f32[9,256,256]{2,1,0:T(8,128)S(1)} %collective-permute-done.7.got_ref), custom_call_target="tpu_custom_call" | custom-call | flops 10000000 | bytes 12000000 | tf_op jit(solution)/shard_map/local_bands/pallas_call | solution.py:187
  52.4 1.8 %collective-permute-done.5.cross_a = f32[136,256]{1,0:T(8,128)S(1)} collective-permute-done((f32[136,256]{1,0:T(8,128)S(1)}, f32[136,256]{1,0:T(8,128)S(1)}, u32[]{:S(2)}, u32[]{:S(2)}) %collective-permute-start.5) | collective-permute-done | bytes 139296 | tf_op jit(solution)/shard_map/ppermute | solution.py:310
  54.2 0.9 %finish.1 = (f32[768,768]{1,0:T(8,128)}, f32[768,512]{1,0:T(8,128)}) custom-call(f32[512,128]{1,0:T(8,128)S(1)} %get-tuple-element.17.sum_a, f32[512,128]{1,0:T(8,128)S(1)} %get-tuple-element.19.sum_b, f32[136,256]{1,0:T(8,128)S(1)} %collective-permute-done.5.cross_a, ...), custom_call_target="tpu_custom_call", output_to_operand_aliasing={{0}: (5, {}), {1}: (6, {})} | custom-call | tf_op jit(solution)/shard_map/finish/pallas_call | solution.py:268
  (5 shorter events, 0.0 us)
Async XLA Ops:
  1.6 31.1 %collective-permute-start.3 = (bf16[512,256]{1,0:T(8,128)(2,1)S(1)}, bf16[512,256]{1,0:T(8,128)(2,1)S(1)}, u32[]{:S(2)}, u32[]{:S(2)}) collective-permute-start(bf16[512,256]{1,0:T(8,128)(2,1)S(1)} %cut_head.1), channel_id=1, source_target_pairs={{0,2},{2,4},{4,6},{6,8},{8,10},{10,12},{12,14},{14,16},{16,18},{18... | collective-permute-start | bytes 786440 | tf_op jit(solution)/shard_map/ppermute | solution.py:298
  4.6 28.6 %collective-permute-start.2 = (bf16[2488,256]{1,0:T(8,128)(2,1)S(1)}, bf16[2488,256]{1,0:T(8,128)(2,1)S(1)}, u32[]{:S(2)}, u32[]{:S(2)}) collective-permute-start(bf16[2488,256]{1,0:T(8,128)(2,1)S(1)} %cut_rest.1), channel_id=1, source_target_pairs={{0,2},{2,4},{4,6},{6,8},{8,10},{10,12},{12,14},{14,16},{16,18},{18... | collective-permute-start | bytes 3821576 | tf_op jit(solution)/shard_map/ppermute | solution.py:299
  9.7 13.0 %copy-start = (s32[6,2]{0,1:T(2,128)S(1)}, s32[6,2]{0,1:T(2,128)}, u32[]{:S(2)}) copy-start(s32[6,2]{0,1:T(2,128)} %param.3) | copy-start | bytes 148
  9.7 26.7 %collective-permute-start.1 = (bf16[3000,512]{1,0:T(8,128)(2,1)}, bf16[3000,512]{1,0:T(8,128)(2,1)S(1)}, u32[]{:S(2)}, u32[]{:S(2)}) collective-permute-start(bf16[3000,512]{1,0:T(8,128)(2,1)} %cut_wide.1), channel_id=1, source_target_pairs={{0,1},{1,0},{2,3},{3,2},{4,5},{5,4},{6,7},{7,6},{8,9},{9,8},{10,11... | collective-permute-start | bytes 9216008 | tf_op jit(solution)/shard_map/ppermute | solution.py:301
  16.7 19.8 %collective-permute-start.4 = (bf16[3000,128]{1,0:T(8,128)(2,1)S(1)}, bf16[3000,128]{1,0:T(8,128)(2,1)S(1)}, u32[]{:S(2)}, u32[]{:S(2)}) collective-permute-start(bf16[3000,128]{1,0:T(8,128)(2,1)S(1)} %get-tuple-element.18), channel_id=1, source_target_pairs={{1,2},{3,4},{5,6},{7,8},{9,10},{11,12},{13,14},{15,16},{17,18},{19... | collective-permute-start | bytes 2304008 | tf_op jit(solution)/shard_map/ppermute | solution.py:300
  16.9 27.8 %collective-permute-start = (bf16[3000,128]{1,0:T(8,128)(2,1)S(1)}, bf16[3000,128]{1,0:T(8,128)(2,1)S(1)}, u32[]{:S(2)}, u32[]{:S(2)}) collective-permute-start(bf16[3000,128]{1,0:T(8,128)(2,1)S(1)} %get-tuple-element.14), channel_id=1, source_target_pairs={{1,2},{3,4},{5,6},{7,8},{9,10},{11,12},{13,14},{15,16},{17,18},{19... | collective-permute-start | bytes 2304008 | tf_op jit(solution)/shard_map/ppermute | solution.py:300
  32.7 17.3 %collective-permute-start.7 = (f32[9,256,256]{2,1,0:T(8,128)S(1)}, f32[9,256,256]{2,1,0:T(8,128)S(1)}, u32[]{:S(2)}, u32[]{:S(2)}) collective-permute-start(f32[9,256,256]{2,1,0:T(8,128)S(1)} %get-tuple-element.23), channel_id=1, source_target_pairs={{0,1},{1,0},{2,3},{3,2},{4,5},{5,4},{6,7},{7,6},{8,9},{9,8},{10,11... | collective-permute-start | bytes 7077896 | tf_op jit(solution)/shard_map/ppermute | solution.py:303
  37.2 15.2 %collective-permute-start.6 = (f32[136,256]{1,0:T(8,128)S(1)}, f32[136,256]{1,0:T(8,128)S(1)}, u32[]{:S(2)}, u32[]{:S(2)}) collective-permute-start(f32[136,256]{1,0:T(8,128)S(1)} %get-tuple-element.21), channel_id=1, source_target_pairs={{1,2},{3,4},{5,6},{7,8},{9,10},{11,12},{13,14},{15,16},{17,18},{19... | collective-permute-start | bytes 417800 | tf_op jit(solution)/shard_map/ppermute | solution.py:310
  45.4 8.8 %collective-permute-start.5 = (f32[136,256]{1,0:T(8,128)S(1)}, f32[136,256]{1,0:T(8,128)S(1)}, u32[]{:S(2)}, u32[]{:S(2)}) collective-permute-start(f32[136,256]{1,0:T(8,128)S(1)} %get-tuple-element.20), channel_id=1, source_target_pairs={{1,2},{3,4},{5,6},{7,8},{9,10},{11,12},{13,14},{15,16},{17,18},{19... | collective-permute-start | bytes 417800 | tf_op jit(solution)/shard_map/ppermute | solution.py:310

commit v7 on v6

--- a/solution.py
+++ b/solution.py
@@ -237,31 +237,39 @@
     near = jnp.where(first, cross_a[HALF:HALF + 1, :HALF], 1.0)
     far = jnp.where(first, cross_a[HALF + 1:HALF + 2, :HALF], 1.0)
     third = jnp.where(first, cross_a[HALF + 2:HALF + 3, :], mask_ref[1:2, :])
-    for half, (sum_ref, cross_ref) in enumerate(((sum_a, cross_a), (sum_b, cross_b))):
-        rows = slice(half * HALF, (half + 1) * HALF)
-        stages[0][:, rows] = jnp.where(near > 0, sum_ref[:BS], 0.0)
-        stages[1][:, rows] = jnp.where(far > 0, sum_ref[BS:], 0.0)
-        stages[2][rows, :] = jnp.where(third > 0, cross_ref[:HALF], 0.0)
-
-    def copies(band, places):
-        moves = [
-            pltpu.make_async_copy(
-                stage, band.at[pl.ds(row * BS, BS), pl.ds(col * BS, BS)], sems.at[i]
-            )
-            for i, (stage, (row, col)) in enumerate(zip(stages, places))
-        ]
-        for move in moves:
-            move.start()
-        for move in moves:
-            move.wait()
+    def move(i, band, place):
+        row, col = place
+        target = band.at[pl.ds(row * BS, BS), pl.ds(col * BS, BS)]
+        return pltpu.make_async_copy(stages[i], target, sems.at[i])
+
+    places = (((0, 0), (1, 2)), ((1, 1), (2, 1)), ((0, 1), (2, 2)))
+    for i, (low, up) in enumerate(places):
+        for half, (sum_ref, cross_ref) in enumerate(((sum_a, cross_a), (sum_b, cross_b))):
+            part = slice(half * HALF, (half + 1) * HALF)
+            if i == 0:
+                stages[0][:, part] = jnp.where(near > 0, sum_ref[:BS], 0.0)
+            elif i == 1:
+                stages[1][:, part] = jnp.where(far > 0, sum_ref[BS:], 0.0)
+            else:
+                stages[2][part, :] = jnp.where(third > 0, cross_ref[:HALF], 0.0)
+
+        @pl.when(first)
+        def _():
+            move(i, lower_ref, low).start()
+
+        @pl.when(core == 1)
+        def _():
+            move(i, upper_ref, up).start()
 
     @pl.when(first)
     def _():
-        copies(lower_ref, ((0, 0), (1, 1), (0, 1)))
+        for i, (low, up) in enumerate(places):
+            move(i, lower_ref, low).wait()
 
     @pl.when(core == 1)
     def _():
-        copies(upper_ref, ((1, 2), (2, 1), (2, 2)))
+        for i, (low, up) in enumerate(places):
+            move(i, upper_ref, up).wait()
 
 
 def finish(sums, crossed, mask, upper, lower):

time: 55.4 us -> 55.3 us (level)
  no operation moved by 1% of the time
where the time goes in v7:
time: 55.3 us; the launch traced here: 55.1 us
  starting transfers between devices  25.5 us (46%)
  Pallas kernels  23 us (42%)
  waiting for transfers between devices  5.89 us (11%)
  between operations  0.74 us (1%)
    ppermute x2, starting transfers between devices, body(): crossed.append(lax.ppermute(send, axes, cross))  10.5 us
    pallas_call x1, Pallas kernels, local_tiles(): pl.pallas_call(local_kernel, in_specs=[SMEM, ANY], out_specs=[VMEM, VMEM,...  9.98 us
    pallas_call x4, Pallas kernels, cut(): pl.pallas_call(functools.partial(cut_kernel, swapped=swapped, skip=skip),...  7.16 us
    ppermute x2, starting transfers between devices, body(): lax.ppermute(piece, axes, cross)  6.05 us
    ppermute x1, starting transfers between devices, body(): other = lax.ppermute(cut('cut_wide', g, 2 * BS, 1, True)[0], axes, swap)  5.52 us
    ppermute x2, waiting for transfers between devices, body(): lax.ppermute(piece, axes, cross)  4.08 us
    pallas_call x1, Pallas kernels, local_bands(): pl.pallas_call(band_kernel, in_specs=[VMEM, VMEM], out_specs=[VMEM, VMEM]...  2.36 us
    ppermute x2, waiting for transfers between devices, body(): crossed.append(lax.ppermute(send, axes, cross))  1.81 us
  transfers between devices with their start and end apart: 8, of which 3 were waited for; matrix products, arithmetic and copies ran while one was open for 0% of the time, Pallas kernels for 38%

profile of v7, /device:TPU:6, one launch (start us, length us, event | category | flops | bytes accessed | tf_op | source)
XLA Modules:
  0.0 55.1 jit_solution(12784894401869593491)
XLA Ops:
  0.6 1.0 %cut_head.1 = bf16[512,256]{1,0:T(8,128)(2,1)S(1)} custom-call(bf16[3000,1536]{1,0:T(8,128)(2,1)} %bitcast.5), custom_call_target="tpu_custom_call" | custom-call | bytes 1000 | tf_op jit(solution)/shard_map/cut_head/pallas_call | solution.py:45
  1.6 1.7 %collective-permute-start.3 = (bf16[512,256]{1,0:T(8,128)(2,1)S(1)}, bf16[512,256]{1,0:T(8,128)(2,1)S(1)}, u32[]{:S(2)}, u32[]{:S(2)}) collective-permute-start(bf16[512,256]{1,0:T(8,128)(2,1)S(1)} %cut_head.1), channel_id=1, source_target_pairs={{0,2},{2,4},{4,6},{6,8},{8,10},{10,12},{12,14},{14,16},{16,18},{18... | collective-permute-start | bytes 786440 | tf_op jit(solution)/shard_map/ppermute | solution.py:306
  3.3 1.3 %cut_rest.1 = bf16[2488,256]{1,0:T(8,128)(2,1)S(1)} custom-call(bf16[3000,1536]{1,0:T(8,128)(2,1)} %bitcast.6), custom_call_target="tpu_custom_call" | custom-call | bytes 1000 | tf_op jit(solution)/shard_map/cut_rest/pallas_call | solution.py:45
  4.6 1.7 %collective-permute-start.2 = (bf16[2488,256]{1,0:T(8,128)(2,1)S(1)}, bf16[2488,256]{1,0:T(8,128)(2,1)S(1)}, u32[]{:S(2)}, u32[]{:S(2)}) collective-permute-start(bf16[2488,256]{1,0:T(8,128)(2,1)S(1)} %cut_rest.1), channel_id=1, source_target_pairs={{0,2},{2,4},{4,6},{6,8},{8,10},{10,12},{12,14},{14,16},{16,18},{18... | collective-permute-start | bytes 3821576 | tf_op jit(solution)/shard_map/ppermute | solution.py:307
  6.2 3.5 %cut_wide.1 = bf16[3000,512]{1,0:T(8,128)(2,1)} custom-call(bf16[3000,1536]{1,0:T(8,128)(2,1)} %bitcast.7), custom_call_target="tpu_custom_call" | custom-call | bytes 1000 | tf_op jit(solution)/shard_map/cut_wide/pallas_call | solution.py:45
  9.7 0.0 copy-start
  9.7 5.5 %collective-permute-start.1 = (bf16[3000,512]{1,0:T(8,128)(2,1)}, bf16[3000,512]{1,0:T(8,128)(2,1)S(1)}, u32[]{:S(2)}, u32[]{:S(2)}) collective-permute-start(bf16[3000,512]{1,0:T(8,128)(2,1)} %cut_wide.1), channel_id=1, source_target_pairs={{0,1},{1,0},{2,3},{3,2},{4,5},{5,4},{6,7},{7,6},{8,9},{9,8},{10,11... | collective-permute-start | bytes 9216008 | tf_op jit(solution)/shard_map/ppermute | solution.py:309
  15.3 1.4 %cut_second.1 = (bf16[3000,128]{1,0:T(8,128)(2,1)S(1)}, bf16[3000,128]{1,0:T(8,128)(2,1)S(1)}) custom-call(bf16[3000,1536]{1,0:T(8,128)(2,1)} %bitcast.8), custom_call_target="tpu_custom_call" | custom-call | bytes 1000 | tf_op jit(solution)/shard_map/cut_second/pallas_call | solution.py:45
  16.7 0.2 collective-permute-start.4
  16.9 5.8 %collective-permute-start = (bf16[3000,128]{1,0:T(8,128)(2,1)S(1)}, bf16[3000,128]{1,0:T(8,128)(2,1)S(1)}, u32[]{:S(2)}, u32[]{:S(2)}) collective-permute-start(bf16[3000,128]{1,0:T(8,128)(2,1)S(1)} %get-tuple-element.14), channel_id=1, source_target_pairs={{1,2},{3,4},{5,6},{7,8},{9,10},{11,12},{13,14},{15,16},{17,18},{19... | collective-permute-start | bytes 2304008 | tf_op jit(solution)/shard_map/ppermute | solution.py:308
  22.7 10.0 %local_tiles.1 = (f32[9,256,256]{2,1,0:T(8,128)S(1)}, f32[9,256,256]{2,1,0:T(8,128)S(1)}, f32[8,256]{1,0:T(8,128)S(1)}, bf16[3000,512]{1,0:T(8,128)(2,1)S(1)}) custom-call(s32[2,6]{1,0:T(2,128)S(1)} %bitcast.4, bf16[3000,1536]{1,0:T(8,128)(2,1)} %bitcast.9), custom_call_target="tpu_custom_call" | custom-call | flops 49999998976 | bytes 1000 | tf_op jit(solution)/shard_map/local_tiles/pallas_call | solution.py:123
  32.7 0.0 collective-permute-done.3.head_ref
  32.7 0.1 collective-permute-start.7
  32.8 0.3 edge_head.1.head_ref
  33.1 0.9 %edge_rest.1.part_ref = f32[256,512]{1,0:T(8,128)S(1)} custom-call(bf16[2488,256]{1,0:T(8,128)(2,1)S(1)} %collective-permute-done.2.rest_ref, bf16[3000,512]{1,0:T(8,128)(2,1)S(1)} %get-tuple-element.15.wide_ref, f32[256,512]{1,0:T(8,128)S(1)} %edge_head.1.head_ref), custom_call_target="tpu_custom_call" | custom-call | bytes 1000 | tf_op jit(solution)/shard_map/edge_rest/pallas_call | solution.py:158
  34.0 2.5 %collective-permute-done.4.came_ref = bf16[3000,128]{1,0:T(8,128)(2,1)S(1)} collective-permute-done((bf16[3000,128]{1,0:T(8,128)(2,1)S(1)}, bf16[3000,128]{1,0:T(8,128)(2,1)S(1)}, u32[]{:S(2)}, u32[]{:S(2)}) %collective-permute-start.4) | collective-permute-done | bytes 768032 | tf_op jit(solution)/shard_map/ppermute | solution.py:308
  36.5 0.7 %edge_sum.3 = (f32[512,128]{1,0:T(8,128)S(1)}, f32[136,256]{1,0:T(8,128)S(1)}) custom-call(bf16[3000,128]{1,0:T(8,128)(2,1)S(1)} %collective-permute-done.4.came_ref, bf16[3000,512]{1,0:T(8,128)(2,1)S(1)} %collective-permute-done.1.wide_ref, f32[256,512]{1,0:T(8,128)S(1)} %edge_rest.1.part_ref, f32[8,256]{1,0:T(8,128)S(1)} %get-tuple-element.16.mask_ref), custom_call_target="tpu_custom_call" | custom-call | flops 49999998976 | bytes 1000 | tf_op jit(solution)/shard_map/edge_sum/pallas_call | solution.py:217
  37.2 5.9 %collective-permute-start.6 = (f32[136,256]{1,0:T(8,128)S(1)}, f32[136,256]{1,0:T(8,128)S(1)}, u32[]{:S(2)}, u32[]{:S(2)}) collective-permute-start(f32[136,256]{1,0:T(8,128)S(1)} %get-tuple-element.21), channel_id=1, source_target_pairs={{1,2},{3,4},{5,6},{7,8},{9,10},{11,12},{13,14},{15,16},{17,18},{19... | collective-permute-start | bytes 417800 | tf_op jit(solution)/shard_map/ppermute | solution.py:318
  43.1 1.6 %collective-permute-done.came_ref = bf16[3000,128]{1,0:T(8,128)(2,1)S(1)} collective-permute-done((bf16[3000,128]{1,0:T(8,128)(2,1)S(1)}, bf16[3000,128]{1,0:T(8,128)(2,1)S(1)}, u32[]{:S(2)}, u32[]{:S(2)}) %collective-permute-start) | collective-permute-done | bytes 768032 | tf_op jit(solution)/shard_map/ppermute | solution.py:308
  44.7 0.7 %edge_sum.2 = (f32[512,128]{1,0:T(8,128)S(1)}, f32[136,256]{1,0:T(8,128)S(1)}) custom-call(bf16[3000,128]{1,0:T(8,128)(2,1)S(1)} %collective-permute-done.came_ref, bf16[3000,512]{1,0:T(8,128)(2,1)S(1)} %collective-permute-done.1.wide_ref, f32[256,512]{1,0:T(8,128)S(1)} %edge_rest.1.part_ref, f32[8,256]{1,0:T(8,128)S(1)} %get-tuple-element.16.mask_ref), custom_call_target="tpu_custom_call" | custom-call | bytes 1000 | tf_op jit(solution)/shard_map/edge_sum/pallas_call | solution.py:217
  45.4 4.6 %collective-permute-start.5 = (f32[136,256]{1,0:T(8,128)S(1)}, f32[136,256]{1,0:T(8,128)S(1)}, u32[]{:S(2)}, u32[]{:S(2)}) collective-permute-start(f32[136,256]{1,0:T(8,128)S(1)} %get-tuple-element.20), channel_id=1, source_target_pairs={{1,2},{3,4},{5,6},{7,8},{9,10},{11,12},{13,14},{15,16},{17,18},{19... | collective-permute-start | bytes 417800 | tf_op jit(solution)/shard_map/ppermute | solution.py:318
  50.0 2.4 %local_bands.1 = (f32[768,768]{1,0:T(8,128)}, f32[768,512]{1,0:T(8,128)}) custom-call(f32[9,256,256]{2,1,0:T(8,128)S(1)} %get-tuple-element.22.keep_ref, f32[9,256,256]{2,1,0:T(8,128)S(1)} %collective-permute-done.7.got_ref), custom_call_target="tpu_custom_call" | custom-call | flops 10000000 | bytes 12000000 | tf_op jit(solution)/shard_map/local_bands/pallas_call | solution.py:187
  52.4 1.8 %collective-permute-done.5.cross_a = f32[136,256]{1,0:T(8,128)S(1)} collective-permute-done((f32[136,256]{1,0:T(8,128)S(1)}, f32[136,256]{1,0:T(8,128)S(1)}, u32[]{:S(2)}, u32[]{:S(2)}) %collective-permute-start.5) | collective-permute-done | bytes 139296 | tf_op jit(solution)/shard_map/ppermute | solution.py:318
  54.2 0.9 %finish.1 = (f32[768,768]{1,0:T(8,128)}, f32[768,512]{1,0:T(8,128)}) custom-call(f32[512,128]{1,0:T(8,128)S(1)} %get-tuple-element.17.sum_a, f32[512,128]{1,0:T(8,128)S(1)} %get-tuple-element.19.sum_b, f32[136,256]{1,0:T(8,128)S(1)} %collective-permute-done.5.cross_a, ...), custom_call_target="tpu_custom_call", output_to_operand_aliasing={{0}: (5, {}), {1}: (6, {})} | custom-call | tf_op jit(solution)/shard_map/finish/pallas_call | solution.py:276
  (5 shorter events, 0.0 us)
Async XLA Ops:
  1.6 31.1 %collective-permute-start.3 = (bf16[512,256]{1,0:T(8,128)(2,1)S(1)}, bf16[512,256]{1,0:T(8,128)(2,1)S(1)}, u32[]{:S(2)}, u32[]{:S(2)}) collective-permute-start(bf16[512,256]{1,0:T(8,128)(2,1)S(1)} %cut_head.1), channel_id=1, source_target_pairs={{0,2},{2,4},{4,6},{6,8},{8,10},{10,12},{12,14},{14,16},{16,18},{18... | collective-permute-start | bytes 786440 | tf_op jit(solution)/shard_map/ppermute | solution.py:306
  4.6 28.6 %collective-permute-start.2 = (bf16[2488,256]{1,0:T(8,128)(2,1)S(1)}, bf16[2488,256]{1,0:T(8,128)(2,1)S(1)}, u32[]{:S(2)}, u32[]{:S(2)}) collective-permute-start(bf16[2488,256]{1,0:T(8,128)(2,1)S(1)} %cut_rest.1), channel_id=1, source_target_pairs={{0,2},{2,4},{4,6},{6,8},{8,10},{10,12},{12,14},{14,16},{16,18},{18... | collective-permute-start | bytes 3821576 | tf_op jit(solution)/shard_map/ppermute | solution.py:307
  9.7 13.0 %copy-start = (s32[6,2]{0,1:T(2,128)S(1)}, s32[6,2]{0,1:T(2,128)}, u32[]{:S(2)}) copy-start(s32[6,2]{0,1:T(2,128)} %param.3) | copy-start | bytes 148
  9.7 26.7 %collective-permute-start.1 = (bf16[3000,512]{1,0:T(8,128)(2,1)}, bf16[3000,512]{1,0:T(8,128)(2,1)S(1)}, u32[]{:S(2)}, u32[]{:S(2)}) collective-permute-start(bf16[3000,512]{1,0:T(8,128)(2,1)} %cut_wide.1), channel_id=1, source_target_pairs={{0,1},{1,0},{2,3},{3,2},{4,5},{5,4},{6,7},{7,6},{8,9},{9,8},{10,11... | collective-permute-start | bytes 9216008 | tf_op jit(solution)/shard_map/ppermute | solution.py:309
  16.7 19.8 %collective-permute-start.4 = (bf16[3000,128]{1,0:T(8,128)(2,1)S(1)}, bf16[3000,128]{1,0:T(8,128)(2,1)S(1)}, u32[]{:S(2)}, u32[]{:S(2)}) collective-permute-start(bf16[3000,128]{1,0:T(8,128)(2,1)S(1)} %get-tuple-element.18), channel_id=1, source_target_pairs={{1,2},{3,4},{5,6},{7,8},{9,10},{11,12},{13,14},{15,16},{17,18},{19... | collective-permute-start | bytes 2304008 | tf_op jit(solution)/shard_map/ppermute | solution.py:308
  16.9 27.8 %collective-permute-start = (bf16[3000,128]{1,0:T(8,128)(2,1)S(1)}, bf16[3000,128]{1,0:T(8,128)(2,1)S(1)}, u32[]{:S(2)}, u32[]{:S(2)}) collective-permute-start(bf16[3000,128]{1,0:T(8,128)(2,1)S(1)} %get-tuple-element.14), channel_id=1, source_target_pairs={{1,2},{3,4},{5,6},{7,8},{9,10},{11,12},{13,14},{15,16},{17,18},{19... | collective-permute-start | bytes 2304008 | tf_op jit(solution)/shard_map/ppermute | solution.py:308
  32.7 17.3 %collective-permute-start.7 = (f32[9,256,256]{2,1,0:T(8,128)S(1)}, f32[9,256,256]{2,1,0:T(8,128)S(1)}, u32[]{:S(2)}, u32[]{:S(2)}) collective-permute-start(f32[9,256,256]{2,1,0:T(8,128)S(1)} %get-tuple-element.23), channel_id=1, source_target_pairs={{0,1},{1,0},{2,3},{3,2},{4,5},{5,4},{6,7},{7,6},{8,9},{9,8},{10,11... | collective-permute-start | bytes 7077896 | tf_op jit(solution)/shard_map/ppermute | solution.py:311
  37.2 15.2 %collective-permute-start.6 = (f32[136,256]{1,0:T(8,128)S(1)}, f32[136,256]{1,0:T(8,128)S(1)}, u32[]{:S(2)}, u32[]{:S(2)}) collective-permute-start(f32[136,256]{1,0:T(8,128)S(1)} %get-tuple-element.21), channel_id=1, source_target_pairs={{1,2},{3,4},{5,6},{7,8},{9,10},{11,12},{13,14},{15,16},{17,18},{19... | collective-permute-start | bytes 417800 | tf_op jit(solution)/shard_map/ppermute | solution.py:318
  45.4 8.8 %collective-permute-start.5 = (f32[136,256]{1,0:T(8,128)S(1)}, f32[136,256]{1,0:T(8,128)S(1)}, u32[]{:S(2)}, u32[]{:S(2)}) collective-permute-start(f32[136,256]{1,0:T(8,128)S(1)} %get-tuple-element.20), channel_id=1, source_target_pairs={{1,2},{3,4},{5,6},{7,8},{9,10},{11,12},{13,14},{15,16},{17,18},{19... | collective-permute-start | bytes 417800 | tf_op jit(solution)/shard_map/ppermute | solution.py:318
